TPU v7x, 512 devices: a whole 4x8x8 slice. The times are simulated.
512 devices in a mesh: grid: 16 (over x, y_lo), orb: 32 (over y_hi, z, core).
Axes of the slice: x: 4, y: 8 (y_hi: 2, y_lo: 4; y = y_hi * 4 + y_lo), z: 8, core: 2. Of those that a mesh axis runs over, the one named last changes fastest.
Arguments:
- orbitals: float32 [256, 4, 384, 256], P('orb', None, 'grid'), may hold values from -6 to 6
- potential: float32 [4, 384, 256], P(None, 'grid'), may hold values from -1.5 to 0
- rotation: bfloat16 [256, 256], replicated, may hold values from -0.375 to 0.375
Outputs:
- rotated: float32 [256, 4, 384, 256], P('orb', None, 'grid')
All inputs are finite; a program needn't handle non-finite values.
Results may differ from a plain program's by a relative error of at most 0.0029.
Values may be sent and summed in bfloat16 or wider, within the bound.
No kernel may reach another device: no remote copies, remote signals or barrier semaphores. Data moves between devices by JAX's collectives and lax.ppermute only.
A program may use at most 64 MiB of HBM per device.

v0:
```python
import jax
import jax.numpy as jnp
from jax import lax
from jax.sharding import PartitionSpec as P

STENCIL = (
    -5369.0 / 1800.0,
    12.0 / 7.0,
    -15.0 / 56.0,
    10.0 / 189.0,
    -1.0 / 112.0,
    2.0 / 1925.0,
    -1.0 / 16632.0,
)
centre_value = 9.0
spread_value = 7.0


def padded_2(cells, sides, width):
    for axis, dim in sides:
        count = lax.axis_size(axis)
        ends = count - 1
        head = lax.slice_in_dim(cells, 0, width, axis=dim)
        tail = lax.slice_in_dim(cells, cells.shape[dim] - width, cells.shape[dim], axis=dim)
        cells = jnp.concatenate(
            [
                lax.ppermute(tail, axis, [(i, (i + 1) % count) for i in range(ends)]),
                cells,
                lax.ppermute(head, axis, [((i + 1) % count, i) for i in range(ends)]),
            ],
            axis=dim,
        )
    return cells


def apply_inner(values, inner_potential):
    inner_width = values.shape[2] - 12
    layers = values.shape[1]
    breadth = values.shape[3]
    centre_cells = values[:, :, 6 : 6 + inner_width]
    side_y = jnp.pad(centre_cells, ((0, 0), (0, 0), (0, 0), (6, 6)))
    side_z = jnp.pad(centre_cells, ((0, 0), (6, 6), (0, 0), (0, 0)))
    summed = 3.0 * STENCIL[0] * centre_cells
    for offset in range(1, 7):
        part_x = (
            values[:, :, 6 + offset : 6 + offset + inner_width]
            + values[:, :, 6 - offset : 6 - offset + inner_width]
        )
        part_y = (
            side_y[:, :, :, 6 + offset : 6 + offset + breadth]
            + side_y[:, :, :, 6 - offset : 6 - offset + breadth]
        )
        part_z = (
            side_z[:, 6 + offset : 6 + offset + layers]
            + side_z[:, 6 - offset : 6 - offset + layers]
        )
        summed = summed + STENCIL[offset] * (part_x + part_y + part_z)
    return -0.5 * summed + inner_potential * centre_cells


def hamiltonian(values, potential):
    padded = padded_2(values, (("grid", 2),), 6)
    return apply_inner(padded, potential)


def chebyshev(values, potential):
    previous = values
    current = (hamiltonian(values, potential) - centre_value * values) / spread_value
    for degree in range(2):
        following = (
            2.0 * (hamiltonian(current, potential) - centre_value * current) / spread_value
            - previous
        )
        previous = current
        current = following
    return current


def local(orbitals, potential, rotation):
    filtered = chebyshev(orbitals, potential)
    filtered = filtered.astype(jnp.bfloat16)
    count, layers, height, breadth = filtered.shape
    cell_count = layers * height * breadth
    flattened = filtered.reshape(count, cell_count)
    own_columns = lax.dynamic_slice_in_dim(rotation, lax.axis_index("orb") * count, count, 1)
    result = jnp.dot(
        own_columns.T,
        lax.all_gather(flattened, "orb", axis=0, tiled=True),
        preferred_element_type=jnp.float32,
    )
    return result.reshape(count, layers, height, breadth)


def solution(mesh):
    return jax.shard_map(
        local,
        mesh=mesh,
        in_specs=(P("orb", None, "grid", None), P(None, "grid", None), P()),
        out_specs=P("orb", None, "grid", None),
        check_vma=False,
    )
```

profile of v0, /device:TPU:6, one launch (start us, length us, event | category | flops | bytes accessed | tf_op | source)
XLA Modules:
  0.0 249.9 jit_solution(10310295565935793886)
XLA Ops:
  6.5 0.0 copy-start
  6.5 0.0 copy-start.1
  6.5 0.0 copy-start.2
  6.5 0.0 all-gather.2.cloned.1.call-start
  6.5 1.2 fusion.153
  7.7 5.8 %collective-permute-start = (f32[8,4,6,256]{3,2,1,0:T(8,128)S(1)}, f32[8,4,6,256]{3,2,1,0:T(8,128)S(1)}, u32[]{:S(2)}, u32[]{:S(2)}) collective-permute-start(f32[8,4,6,256]{3,2,1,0:T(8,128)S(1)} %get-tuple-element.11), channel_id=1, source_target_pairs={{32,0},{64,32},{96,64},{128,96},{160,128},{192,160},{224,192},{256... | collective-permute-start | bytes 589832 | tf_op jit(solution)/shard_map/ppermute | solution.py:29
  13.5 1.9 collective-permute-start.1
  15.4 1.2 constant_dynamic-update-slice_fusion.1
  16.6 3.6 %collective-permute-done = f32[8,4,6,256]{3,2,1,0:T(8,128)S(1)} collective-permute-done((f32[8,4,6,256]{3,2,1,0:T(8,128)S(1)}, f32[8,4,6,256]{3,2,1,0:T(8,128)S(1)}, u32[]{:S(2)}, u32[]{:S(2)}) %collective-permute-start) | collective-permute-done | bytes 196640 | tf_op jit(solution)/shard_map/ppermute | solution.py:29
  20.3 5.6 %collective-permute-done.1 = f32[8,4,6,256]{3,2,1,0:T(8,128)S(1)} collective-permute-done((f32[8,4,6,256]{3,2,1,0:T(8,128)S(1)}, f32[8,4,6,256]{3,2,1,0:T(8,128)S(1)}, u32[]{:S(2)}, u32[]{:S(2)}) %collective-permute-start.1) | collective-permute-done | bytes 196640 | tf_op jit(solution)/shard_map/ppermute | solution.py:27
  25.9 0.0 copy-done.1
  25.9 0.0 copy-done.2
  25.9 2.6 %broadcast_multiply_fusion = (f32[8,4,24,256]{3,2,1,0:T(8,128)S(1)}, f32[8,4,24,256]{3,2,1,0:T(8,128)S(1)}) fusion(f32[8,4,24,256]{3,2,1,0:T(8,128)S(1)} %copy-done.1, f32[4,24,256]{2,1,0:T(8,128)S(1)} %copy-done.2, f32[8,4,6,256]{3,2,1,0:T(8,128)S(1)} %collective-permute-done.1, f32[8,4,30,256]{3,2,1,0:T(8,128)S(1)} %constant_dynamic-update-slice_fusion), kind=kLoop, calls=%fused_computation.256 | loop fusion | flops 9633792 | bytes 7372800 | tf_op jit(solution)/shard_map/div | solution.py:68
  28.5 5.0 %collective-permute-start.2 = (f32[8,4,6,256]{3,2,1,0:T(8,128)S(1)}, f32[8,4,6,256]{3,2,1,0:T(8,128)S(1)}, u32[]{:S(2)}, u32[]{:S(2)}) collective-permute-start(f32[8,4,6,256]{3,2,1,0:T(8,128)S(1)} %get-tuple-element.9), channel_id=1, source_target_pairs={{32,0},{64,32},{96,64},{128,96},{160,128},{192,160},{224,192},{256... | collective-permute-start | bytes 589832 | tf_op jit(solution)/shard_map/ppermute | solution.py:29
  33.5 1.9 collective-permute-start.3
  35.5 4.8 %collective-permute-done.2 = f32[8,4,6,256]{3,2,1,0:T(8,128)S(1)} collective-permute-done((f32[8,4,6,256]{3,2,1,0:T(8,128)S(1)}, f32[8,4,6,256]{3,2,1,0:T(8,128)S(1)}, u32[]{:S(2)}, u32[]{:S(2)}) %collective-permute-start.2) | collective-permute-done | bytes 196640 | tf_op jit(solution)/shard_map/ppermute | solution.py:29
  40.2 5.8 %collective-permute-done.3 = f32[8,4,6,256]{3,2,1,0:T(8,128)S(1)} collective-permute-done((f32[8,4,6,256]{3,2,1,0:T(8,128)S(1)}, f32[8,4,6,256]{3,2,1,0:T(8,128)S(1)}, u32[]{:S(2)}, u32[]{:S(2)}) %collective-permute-start.3) | collective-permute-done | bytes 196640 | tf_op jit(solution)/shard_map/ppermute | solution.py:27
  46.0 2.8 %fusion.49 = f32[8,4,24,256]{3,2,1,0:T(8,128)S(1)} fusion(f32[8,4,24,256]{3,2,1,0:T(8,128)S(1)} %copy-done.1, f32[8,4,24,256]{3,2,1,0:T(8,128)S(1)} %get-tuple-element.5, f32[8,4,6,256]{3,2,1,0:T(8,128)S(1)} %collective-permute-done.3, f32[8,4,6,256]{3,2,1,0:T(8,128)S(1)} %collective-permute-done.2, f32[8,4,24,256]{3,2,1,0:T(8,128)S(1)} %get-tuple-element.6, ...), kind=kLoop, calls=%fused_computation.153 | loop fusion | flops 11010048 | bytes 3637248 | tf_op jit(solution)/shard_map/sub | solution.py:71
  48.8 5.0 %collective-permute-start.4 = (f32[8,4,6,256]{3,2,1,0:T(8,128)S(1)}, f32[8,4,6,256]{3,2,1,0:T(8,128)S(1)}, u32[]{:S(2)}, u32[]{:S(2)}) collective-permute-start(f32[8,4,6,256]{3,2,1,0:T(8,128)S(1)} %get-tuple-element.7), channel_id=1, source_target_pairs={{32,0},{64,32},{96,64},{128,96},{160,128},{192,160},{224,192},{256... | collective-permute-start | bytes 589832 | tf_op jit(solution)/shard_map/ppermute | solution.py:29
  53.8 1.9 collective-permute-start.5
  55.7 4.8 %collective-permute-done.4 = f32[8,4,6,256]{3,2,1,0:T(8,128)S(1)} collective-permute-done((f32[8,4,6,256]{3,2,1,0:T(8,128)S(1)}, f32[8,4,6,256]{3,2,1,0:T(8,128)S(1)}, u32[]{:S(2)}, u32[]{:S(2)}) %collective-permute-start.4) | collective-permute-done | bytes 196640 | tf_op jit(solution)/shard_map/ppermute | solution.py:29
  60.5 5.8 %collective-permute-done.5 = f32[8,4,6,256]{3,2,1,0:T(8,128)S(1)} collective-permute-done((f32[8,4,6,256]{3,2,1,0:T(8,128)S(1)}, f32[8,4,6,256]{3,2,1,0:T(8,128)S(1)}, u32[]{:S(2)}, u32[]{:S(2)}) %collective-permute-start.5) | collective-permute-done | bytes 196640 | tf_op jit(solution)/shard_map/ppermute | solution.py:27
  66.3 2.8 %fusion.146 = bf16[8,4,24,256]{3,2,1,0:T(8,128)(2,1)S(1)} fusion(f32[8,4,24,256]{3,2,1,0:T(8,128)S(1)} %fusion.49, f32[8,4,6,256]{3,2,1,0:T(8,128)S(1)} %collective-permute-done.5, f32[8,4,6,256]{3,2,1,0:T(8,128)S(1)} %collective-permute-done.4, f32[8,4,24,256]{3,2,1,0:T(8,128)S(1)} %get-tuple-element.6, f32[4,24,256]{2,1,0:T(8,128)S(1)} %copy-done.2), kind=kLoop, calls=%fused_computation.255 | loop fusion | flops 11403264 | bytes 2457600 | tf_op jit(solution)/shard_map/convert_element_type | solution.py:81
  69.1 1.0 copy.5
  70.1 0.0 all-gather.2.cloned.1.call-update
  70.1 165.4 %all-gather.2.cloned.1.call-done = bf16[256,24576]{1,0:T(8,128)(2,1)} async-done(((bf16[8,24576]{1,0:T(8,128)(2,1)}), bf16[256,24576]{1,0:T(8,128)(2,1)}) %all-gather.2.cloned.1.call-update) | async-done | bytes 12582928 | tf_op jit(solution)/shard_map/all_gather | solution.py:88
  235.5 0.0 copy-done
  235.5 6.4 %fusion.147 = f32[8,24576]{1,0:T(8,128)S(1)} fusion(bf16[256,24576]{1,0:T(8,128)(2,1)} %all-gather.2.cloned.1.call-done, bf16[256,256]{1,0:T(8,128)(2,1)S(1)} %copy-done, s32[]{:T(128)S(6)} %select_n.3), kind=kOutput, calls=%fused_computation.257 | convolution fusion | flops 100663296 | bytes 13434884 | tf_op jit(solution)/shard_map/dot_general | solution.py:86
  241.9 1.1 copy.4
  (4 shorter events, 0.1 us)
Async XLA Ops:
  6.5 229.0 %copy-start = (bf16[256,256]{1,0:T(8,128)(2,1)S(1)}, bf16[256,256]{1,0:T(8,128)(2,1)}, u32[]{:S(2)}) copy-start(bf16[256,256]{1,0:T(8,128)(2,1)} %param.5) | copy-start | bytes 393220
  6.5 19.3 %copy-start.1 = (f32[8,4,24,256]{3,2,1,0:T(8,128)S(1)}, f32[8,4,24,256]{3,2,1,0:T(8,128)}, u32[]{:S(2)}) copy-start(f32[8,4,24,256]{3,2,1,0:T(8,128)} %param.3) | copy-start | bytes 2359300
  6.5 19.3 %copy-start.2 = (f32[4,24,256]{2,1,0:T(8,128)S(1)}, f32[4,24,256]{2,1,0:T(8,128)}, u32[]{:S(2)}) copy-start(f32[4,24,256]{2,1,0:T(8,128)} %param.4) | copy-start | bytes 294916
  6.5 229.0 %all-gather.2.cloned.1.call-start = ((), (), s32[]{:S(2)}) async-start(), calls=%async_computation | async-start | bytes 12976128 | tf_op jit(solution)/shard_map/all_gather | solution.py:88
  7.7 12.5 %collective-permute-start = (f32[8,4,6,256]{3,2,1,0:T(8,128)S(1)}, f32[8,4,6,256]{3,2,1,0:T(8,128)S(1)}, u32[]{:S(2)}, u32[]{:S(2)}) collective-permute-start(f32[8,4,6,256]{3,2,1,0:T(8,128)S(1)} %get-tuple-element.11), channel_id=1, source_target_pairs={{32,0},{64,32},{96,64},{128,96},{160,128},{192,160},{224,192},{256... | collective-permute-start | bytes 589832 | tf_op jit(solution)/shard_map/ppermute | solution.py:29
  13.5 12.4 %collective-permute-start.1 = (f32[8,4,6,256]{3,2,1,0:T(8,128)S(1)}, f32[8,4,6,256]{3,2,1,0:T(8,128)S(1)}, u32[]{:S(2)}, u32[]{:S(2)}) collective-permute-start(f32[8,4,6,256]{3,2,1,0:T(8,128)S(1)} %get-tuple-element.12), channel_id=1, source_target_pairs={{0,32},{32,64},{64,96},{96,128},{128,160},{160,192},{192,224},{224... | collective-permute-start | bytes 589832 | tf_op jit(solution)/shard_map/ppermute | solution.py:27
  28.5 11.7 %collective-permute-start.2 = (f32[8,4,6,256]{3,2,1,0:T(8,128)S(1)}, f32[8,4,6,256]{3,2,1,0:T(8,128)S(1)}, u32[]{:S(2)}, u32[]{:S(2)}) collective-permute-start(f32[8,4,6,256]{3,2,1,0:T(8,128)S(1)} %get-tuple-element.9), channel_id=1, source_target_pairs={{32,0},{64,32},{96,64},{128,96},{160,128},{192,160},{224,192},{256... | collective-permute-start | bytes 589832 | tf_op jit(solution)/shard_map/ppermute | solution.py:29
  33.5 12.5 %collective-permute-start.3 = (f32[8,4,6,256]{3,2,1,0:T(8,128)S(1)}, f32[8,4,6,256]{3,2,1,0:T(8,128)S(1)}, u32[]{:S(2)}, u32[]{:S(2)}) collective-permute-start(f32[8,4,6,256]{3,2,1,0:T(8,128)S(1)} %get-tuple-element.10), channel_id=1, source_target_pairs={{0,32},{32,64},{64,96},{96,128},{128,160},{160,192},{192,224},{224... | collective-permute-start | bytes 589832 | tf_op jit(solution)/shard_map/ppermute | solution.py:27
  48.8 11.7 %collective-permute-start.4 = (f32[8,4,6,256]{3,2,1,0:T(8,128)S(1)}, f32[8,4,6,256]{3,2,1,0:T(8,128)S(1)}, u32[]{:S(2)}, u32[]{:S(2)}) collective-permute-start(f32[8,4,6,256]{3,2,1,0:T(8,128)S(1)} %get-tuple-element.7), channel_id=1, source_target_pairs={{32,0},{64,32},{96,64},{128,96},{160,128},{192,160},{224,192},{256... | collective-permute-start | bytes 589832 | tf_op jit(solution)/shard_map/ppermute | solution.py:29
  53.8 12.5 %collective-permute-start.5 = (f32[8,4,6,256]{3,2,1,0:T(8,128)S(1)}, f32[8,4,6,256]{3,2,1,0:T(8,128)S(1)}, u32[]{:S(2)}, u32[]{:S(2)}) collective-permute-start(f32[8,4,6,256]{3,2,1,0:T(8,128)S(1)} %get-tuple-element.8), channel_id=1, source_target_pairs={{0,32},{32,64},{64,96},{96,128},{128,160},{160,192},{192,224},{224... | collective-permute-start | bytes 589832 | tf_op jit(solution)/shard_map/ppermute | solution.py:27
Sparse Core Ops, SparseCore 0:
  70.2 165.2 all-gather.1
where the time goes:
time: 252 us; the launch traced here: 250 us
  waiting for transfers between devices  196 us (78%)
  starting transfers between devices  21.5 us (9%)
  between operations  13.5 us (5%)
  other arithmetic  8.17 us (3%)
  matrix products  6.41 us (3%)
  local copies, waits for them, and re-layouts  4.58 us (2%)
    all_gather x1, waiting for transfers between devices, local(): lax.all_gather(flattened, 'orb', axis=0, tiled=True)  165 us
    ppermute x3, waiting for transfers between devices, padded_2(): lax.ppermute(tail, axis, [(i, (i + 1) % count) for i in range(ends)])  17.1 us
    ppermute x3, starting transfers between devices, padded_2(): lax.ppermute(head, axis, [((i + 1) % count, i) for i in range(ends)])  15.7 us
    ppermute x3, waiting for transfers between devices, padded_2(): lax.ppermute(head, axis, [((i + 1) % count, i) for i in range(ends)])  13.2 us
    dot_general x1, matrix products, local(): jnp.dot(own_columns.T, lax.all_gather(flattened, 'orb', axis=0, tiled=Tru...  6.41 us
    ppermute x3, starting transfers between devices, padded_2(): lax.ppermute(tail, axis, [(i, (i + 1) % count) for i in range(ends)])  5.76 us
  transfers between devices with their start and end apart: 7, of which 7 were waited for; matrix products, arithmetic and copies ran while one was open for 0% of the time, Pallas kernels for 0%

commit v1 on v0

v1 whole, which is shorter than its diff:
```python
import jax
import jax.numpy as jnp
import numpy as np
from jax import lax
from jax.experimental import pallas as pl
from jax.experimental.pallas import tpu as pltpu
from jax.sharding import PartitionSpec as P

STENCIL = (
    -5369.0 / 1800.0,
    12.0 / 7.0,
    -15.0 / 56.0,
    10.0 / 189.0,
    -1.0 / 112.0,
    2.0 / 1925.0,
    -1.0 / 16632.0,
)
CENTRE = 9.0
SPREAD = 7.0
REACH = 6
TAPS = tuple(-0.5 * s / SPREAD for s in STENCIL)
DIAGONAL = (-CENTRE - 1.5 * STENCIL[0]) / SPREAD
VMEM_LIMIT = 40 * 1024 * 1024
WHOLE = pl.BlockSpec(memory_space=pltpu.VMEM)


def band_matrix(breadth):
    band = np.zeros((breadth, breadth), np.float64)
    for offset in range(1, REACH + 1):
        band += TAPS[offset] * (np.eye(breadth, k=offset) + np.eye(breadth, k=-offset))
    high = band.astype(jnp.bfloat16)
    low = (band - high.astype(np.float64)).astype(jnp.bfloat16)
    return np.stack([high, low])


def call(kernel, out_shape, *args, scratch=(), flops=0, **kwargs):
    moved = sum(a.size * a.dtype.itemsize for a in args)
    return pl.pallas_call(
        kernel,
        out_shape=out_shape,
        in_specs=[WHOLE] * len(args),
        out_specs=jax.tree.map(lambda _: WHOLE, out_shape),
        scratch_shapes=list(scratch),
        compiler_params=pltpu.CompilerParams(vmem_limit_bytes=VMEM_LIMIT),
        cost_estimate=pl.CostEstimate(flops=flops, bytes_accessed=moved, transcendentals=0),
        **kwargs,
    )(*args)


def pack(orbitals, potential, count, layers, height):
    breadth = orbitals.shape[2]
    halo, near = 3 * REACH, 2 * REACH
    rows = layers * halo * count + layers * near

    def kernel(x_ref, p_ref, own_ref, head_ref, tail_ref):
        for layer in range(layers):
            own = jnp.concatenate(
                [
                    jnp.swapaxes(x_ref[:, layer * height + r : layer * height + r + 8, :], 0, 1)
                    for r in range(0, height, 8)
                ],
                axis=0,
            )
            own_ref[layer * height * count : (layer + 1) * height * count, :] = own.reshape(-1, breadth)
            here = slice(layer * halo * count, (layer + 1) * halo * count)
            head_ref[here, :] = own[:halo].reshape(-1, breadth).astype(jnp.bfloat16)
            tail_ref[here, :] = own[height - halo :].reshape(-1, breadth).astype(jnp.bfloat16)
        for out_ref, first in ((head_ref, 0), (tail_ref, height - near)):
            strips = [
                p_ref[layer * height + first : layer * height + first + near, :] for layer in range(layers)
            ]
            out_ref[layers * halo * count :, :] = jnp.concatenate(strips, axis=0).astype(jnp.bfloat16)

    shape = jax.ShapeDtypeStruct((rows, breadth), jnp.bfloat16)
    own = jax.ShapeDtypeStruct((layers * height * count, breadth), jnp.float32)
    return call(kernel, (own, shape, shape), orbitals, potential)


def filtering(own, potential, before, after, inside, count, layers, height):
    breadth = own.shape[1]
    halo, near = 3 * REACH, 2 * REACH
    tall = (height + 2 * halo, height + 2 * near, height + 2 * REACH, height)

    def kernel(x_ref, p_ref, before_ref, after_ref, band_ref, inside_ref, out_ref, v0, d1, d2, w):
        for layer in range(layers):
            base = layer * tall[0] * count
            source = slice(layer * halo * count, (layer + 1) * halo * count)
            v0[base : base + halo * count, :] = before_ref[source, :].astype(jnp.float32)
            base += (halo + height) * count
            v0[base : base + halo * count, :] = after_ref[source, :].astype(jnp.float32)
            base -= height * count
            v0[base : base + height * count, :] = x_ref[
                layer * height * count : (layer + 1) * height * count, :
            ]
        strips = layers * halo * count
        for layer in range(layers):
            base = layer * tall[1]
            source = slice(strips + layer * near, strips + (layer + 1) * near)
            w[base : base + near, :] = before_ref[source, :].astype(jnp.float32) * (1.0 / SPREAD) + DIAGONAL
            w[base + near : base + near + height, :] = (
                p_ref[layer * height : (layer + 1) * height, :] * (1.0 / SPREAD) + DIAGONAL
            )
            base += near + height
            w[base : base + near, :] = after_ref[source, :].astype(jnp.float32) * (1.0 / SPREAD) + DIAGONAL

        high, low = band_ref[0], band_ref[1]

        def along_y(src, src_tall, layer, dst_tall):
            start = (layer * src_tall + REACH) * count
            u = src[start : start + dst_tall * count, :]
            u_high = u.astype(jnp.bfloat16)
            u_low = (u - u_high.astype(jnp.float32)).astype(jnp.bfloat16)

            def dot(a, b):
                return jnp.dot(a, b, preferred_element_type=jnp.float32)

            return dot(u_high, high) + (dot(u_low, high) + dot(u_high, low))

        def stage(number, src, dst, previous):
            src_tall, dst_tall = tall[number - 1], tall[number]
            outer = (dst_tall - height) // 2
            for layer in range(layers):
                dst[layer * dst_tall * count : (layer + 1) * dst_tall * count, :] = along_y(
                    src, src_tall, layer, dst_tall
                )
            blocks = dst_tall // REACH

            def step(b, carry):
                if outer:
                    keep = jnp.where(
                        b < outer // REACH,
                        inside_ref[0],
                        jnp.where(b >= blocks - outer // REACH, inside_ref[1], 1.0),
                    )
                centres = []
                for layer in range(layers):
                    first = (layer * src_tall + b * REACH + REACH) * count
                    first = pl.multiple_of(first, 8)
                    centres.append(src[pl.ds(first, REACH * count), :].reshape(REACH, count, breadth))
                for layer in range(layers):
                    first = pl.multiple_of((layer * src_tall + b * REACH) * count, 8)
                    u = src[pl.ds(first, 3 * REACH * count), :].reshape(3 * REACH, count, breadth)
                    place = pl.multiple_of((layer * dst_tall + b * REACH) * count, 8)
                    here = pl.ds(place, REACH * count)
                    total = dst[here, :].reshape(REACH, count, breadth)
                    w_first = layer * tall[1] + (near - outer) + b * REACH
                    diagonal = jnp.stack(
                        [
                            jnp.broadcast_to(w[pl.ds(w_first + r, 1), :], (count, breadth))
                            for r in range(REACH)
                        ]
                    )
                    total = total + diagonal * centres[layer]
                    for offset in range(1, REACH + 1):
                        pair = u[REACH - offset : 2 * REACH - offset] + u[REACH + offset : 2 * REACH + offset]
                        if offset < layers:
                            if layer - offset >= 0:
                                pair = pair + centres[layer - offset]
                            if layer + offset < layers:
                                pair = pair + centres[layer + offset]
                        total = total + TAPS[offset] * pair
                    if number > 1:
                        prev_tall = tall[number - 2]
                        p_first = (layer * prev_tall + b * REACH + 2 * REACH) * count
                        p_first = pl.multiple_of(p_first, 8)
                        before_last = previous[pl.ds(p_first, REACH * count), :].reshape(
                            REACH, count, breadth
                        )
                        total = 2.0 * total - before_last
                    if outer:
                        total = total * keep
                    total = total.reshape(REACH * count, breadth)
                    if number == 3:
                        out_ref[here, :] = total.astype(jnp.bfloat16)
                    else:
                        dst[here, :] = total
                return carry

            lax.fori_loop(0, blocks, step, 0)

        stage(1, v0, d1, None)
        stage(2, d1, d2, v0)
        stage(3, d2, v0, d1)

    scratch = [pltpu.VMEM((layers * t * count, breadth), jnp.float32) for t in tall[:3]]
    scratch.append(pltpu.VMEM((layers * tall[1], breadth), jnp.float32))
    band = jnp.asarray(band_matrix(breadth))
    return pl.pallas_call(
        kernel,
        out_shape=jax.ShapeDtypeStruct((layers * height * count, breadth), jnp.bfloat16),
        in_specs=[WHOLE] * 5 + [pl.BlockSpec(memory_space=pltpu.SMEM)],
        out_specs=WHOLE,
        scratch_shapes=scratch,
        compiler_params=pltpu.CompilerParams(vmem_limit_bytes=VMEM_LIMIT),
        cost_estimate=pl.CostEstimate(flops=2 * 3456 * 256 * 768, bytes_accessed=3 << 20, transcendentals=0),
    )(own, potential, before, after, band, inside)


def rotate(blocks, rotation, parts, per, count):
    rows, breadth = blocks.shape
    total = parts * count

    def kernel(g_ref, r_ref, out_ref):
        cells = g_ref[...].astype(jnp.float32).reshape(parts, per, count, breadth)
        turn = r_ref[...]
        outs = []
        for r in range(per):
            part = cells[:, r].reshape(total, breadth).astype(jnp.bfloat16)
            product = lax.dot_general(
                turn, part, (((0,), (0,)), ((), ())), preferred_element_type=jnp.float32
            )
            outs.append(product.reshape(parts, 1, count, breadth))
        result = jnp.concatenate(outs, axis=1).reshape(rows, breadth)
        out_ref[...] = result.astype(jnp.bfloat16)

    return call(
        kernel,
        jax.ShapeDtypeStruct((rows, breadth), jnp.bfloat16),
        blocks,
        rotation,
        flops=2 * total * rows * breadth,
    )


def unpack(rows, count, cells):
    breadth = rows.shape[1]

    def kernel(q_ref, out_ref):
        for first in range(0, cells, 8):
            group = q_ref[first * count : (first + 8) * count, :].astype(jnp.float32)
            out_ref[:, first : first + 8, :] = jnp.swapaxes(group.reshape(8, count, breadth), 0, 1)

    return call(kernel, jax.ShapeDtypeStruct((count, cells, breadth), jnp.float32), rows)


def local(orbitals, potential, rotation):
    count, layers, height, breadth = orbitals.shape
    cells = layers * height
    parts = lax.axis_size("orb")
    columns = lax.axis_size("grid")
    orbitals = orbitals.reshape(count, cells, breadth)
    potential = potential.reshape(cells, breadth)
    own, head, tail = pack(orbitals, potential, count, layers, height)
    before = lax.ppermute(tail, "grid", [(i, i + 1) for i in range(columns - 1)])
    after = lax.ppermute(head, "grid", [(i + 1, i) for i in range(columns - 1)])
    place = lax.axis_index("grid")
    inside = jnp.stack([place > 0, place < columns - 1]).astype(jnp.float32)
    filtered = filtering(own, potential, before, after, inside, count, layers, height)
    per = cells // parts
    filtered = filtered.reshape(parts, per * count, breadth)
    gathered = lax.all_to_all(filtered, "orb", 0, 0, tiled=True)
    rotated = rotate(gathered.reshape(cells * count, breadth), rotation, parts, per, count)
    returned = lax.all_to_all(rotated.reshape(parts, per * count, breadth), "orb", 0, 0, tiled=True)
    result = unpack(returned.reshape(cells * count, breadth), count, cells)
    return result.reshape(count, layers, height, breadth)


def solution(mesh):
    return jax.shard_map(
        local,
        mesh=mesh,
        in_specs=(P("orb", None, "grid", None), P(None, "grid", None), P()),
        out_specs=P("orb", None, "grid", None),
        check_vma=False,
    )
```

time: 252 us -> 87.4 us (0.35)
  the two profiles are of different devices: /device:TPU:6 before, /device:TPU:18 now
where the time goes in v1:
time: 87.4 us; the launch traced here: 87.1 us
  blocking collectives  59 us (68%)
  waiting for transfers between devices  12.8 us (15%)
  Pallas kernels  7.31 us (8%)
  starting transfers between devices  5.84 us (7%)
  local copies, waits for them, and re-layouts  2.04 us (2%)
    all_to_all x1, blocking collectives, local(): gathered = lax.all_to_all(filtered, 'orb', 0, 0, tiled=True)  35.9 us
    all_to_all x1, blocking collectives, local(): lax.all_to_all(rotated.reshape(parts, per * count, breadth), 'orb', 0, 0,...  23.1 us
    ppermute x1, waiting for transfers between devices, local(): lax.ppermute(tail, 'grid', [(i, i + 1) for i in range(columns - 1)])  12.1 us
    pallas_call x1, Pallas kernels, filtering(): pl.pallas_call(kernel, out_shape=jax.ShapeDtypeStruct((layers * height *...  5.8 us
    ppermute x1, starting transfers between devices, local(): lax.ppermute(tail, 'grid', [(i, i + 1) for i in range(columns - 1)])  3.48 us
    ppermute x1, starting transfers between devices, local(): after = lax.ppermute(head, 'grid', [(i + 1, i) for i in range(columns - 1)])  2.36 us
    unnamed x10, local copies, waits for them, and re-layouts  2.04 us
  transfers between devices with their start and end apart: 2, of which 2 were waited for; matrix products, arithmetic and copies ran while one was open for 0% of the time, Pallas kernels for 0%

profile of v1, /device:TPU:18, one launch (start us, length us, event | category | flops | bytes accessed | tf_op | source)
XLA Modules:
  0.0 87.1 jit_solution(4470893316148767915)
XLA Ops:
  0.0 0.0 copy-start
  0.0 1.1 %copy-done = f32[8,4,24,256]{3,2,1,0:T(8,128)S(1)} copy-done((f32[8,4,24,256]{3,2,1,0:T(8,128)S(1)}, f32[8,4,24,256]{3,2,1,0:T(8,128)}, u32[]{:S(2)}) %copy-start) | copy-done | bytes 786456
  1.1 0.0 copy-start.2
  1.1 0.9 %copy-done.2 = f32[4,24,256]{2,1,0:T(8,128)S(1)} copy-done((f32[4,24,256]{2,1,0:T(8,128)S(1)}, f32[4,24,256]{2,1,0:T(8,128)}, u32[]{:S(2)}) %copy-start.2) | copy-done | bytes 98328
  2.0 0.0 copy-start.3
  2.0 0.0 copy-start.4
  2.0 0.2 shard_map.46
  2.2 3.5 %collective-permute-start = (bf16[624,256]{1,0:T(8,128)(2,1)S(1)}, bf16[624,256]{1,0:T(8,128)(2,1)S(1)}, u32[]{:S(2)}, u32[]{:S(2)}) collective-permute-start(bf16[624,256]{1,0:T(8,128)(2,1)S(1)} %get-tuple-element.9), channel_id=1, source_target_pairs={{0,32},{32,64},{64,96},{96,128},{128,160},{160,192},{192,224},{224... | collective-permute-start | bytes 958472 | tf_op jit(solution)/shard_map/ppermute | solution.py:244
  5.7 2.4 %collective-permute-start.1 = (bf16[624,256]{1,0:T(8,128)(2,1)S(1)}, bf16[624,256]{1,0:T(8,128)(2,1)S(1)}, u32[]{:S(2)}, u32[]{:S(2)}) collective-permute-start(bf16[624,256]{1,0:T(8,128)(2,1)S(1)} %get-tuple-element.10), channel_id=1, source_target_pairs={{32,0},{64,32},{96,64},{128,96},{160,128},{192,160},{224,192},{256... | collective-permute-start | bytes 958472 | tf_op jit(solution)/shard_map/ppermute | solution.py:245
  8.1 0.1 add_convert_fusion.inside_ref
  8.2 12.1 %collective-permute-done.before_ref = bf16[624,256]{1,0:T(8,128)(2,1)S(1)} collective-permute-done((bf16[624,256]{1,0:T(8,128)(2,1)S(1)}, bf16[624,256]{1,0:T(8,128)(2,1)S(1)}, u32[]{:S(2)}, u32[]{:S(2)}) %collective-permute-start) | collective-permute-done | bytes 319520 | tf_op jit(solution)/shard_map/ppermute | solution.py:244
  20.2 0.7 collective-permute-done.1.after_ref
  21.0 0.0 copy-done.3
  21.0 0.0 copy-done.4
  21.0 5.8 %shard_map.47 = bf16[768,256]{1,0:T(8,128)(2,1)S(1)} custom-call(f32[768,256]{1,0:T(8,128)S(1)} %get-tuple-element.8.x_ref, f32[96,256]{1,0:T(8,128)S(1)} %bitcast.15, bf16[624,256]{1,0:T(8,128)(2,1)S(1)} %collective-permute-done.before_ref, bf16[624,256]{1,0:T(8,128)(2,1)S(1)} %collective-permute-done.1.after_ref, bf16[2,256,256]{2,1,0:T(8,128)(2,1)S(1)} %copy-done.4, ...), custom_call_target="tpu_custom_call" | custom-call | flops 1358954496 | bytes 3145728 | tf_op jit(solution)/shard_map/pallas_call | solution.py:188
  26.8 0.0 copy-start.1
  26.8 35.9 %all_to_all.10 = bf16[32,24,256]{2,1,0:T(8,128)(2,1)S(1)} all-to-all(bf16[32,24,256]{2,1,0:T(8,128)(2,1)S(1)} %bitcast.13), channel_id=1, replica_groups=mesh['grid'=16,'orb'=32] {'orb'}, dimensions={0} | all-to-all | bytes 786432 | tf_op jit(solution)/shard_map/all_to_all | solution.py:251
  62.7 0.0 copy-done.1
  62.7 0.3 shard_map.48
  63.0 23.1 %all_to_all.11 = bf16[32,24,256]{2,1,0:T(8,128)(2,1)S(1)} all-to-all(bf16[32,24,256]{2,1,0:T(8,128)(2,1)S(1)} %bitcast.10), channel_id=1, replica_groups=mesh['grid'=16,'orb'=32] {'orb'}, dimensions={0} | all-to-all | bytes 786432 | tf_op jit(solution)/shard_map/all_to_all | solution.py:253
  86.1 1.0 %shard_map.49 = f32[8,96,256]{2,1,0:T(8,128)} custom-call(bf16[768,256]{1,0:T(8,128)(2,1)S(1)} %bitcast.11), custom_call_target="tpu_custom_call" | custom-call | bytes 393216 | tf_op jit(solution)/shard_map/pallas_call | solution.py:38
Async XLA Ops:
  0.0 1.1 %copy-start = (f32[8,4,24,256]{3,2,1,0:T(8,128)S(1)}, f32[8,4,24,256]{3,2,1,0:T(8,128)}, u32[]{:S(2)}) copy-start(f32[8,4,24,256]{3,2,1,0:T(8,128)} %param.4) | copy-start | bytes 2359300
  1.1 0.9 %copy-start.2 = (f32[4,24,256]{2,1,0:T(8,128)S(1)}, f32[4,24,256]{2,1,0:T(8,128)}, u32[]{:S(2)}) copy-start(f32[4,24,256]{2,1,0:T(8,128)} %param.5) | copy-start | bytes 294916
  2.0 18.9 %copy-start.3 = (f32[4,24,256]{2,1,0:T(8,128)S(1)}, f32[4,24,256]{2,1,0:T(8,128)}, u32[]{:S(2)}) copy-start(f32[4,24,256]{2,1,0:T(8,128)} %param.5) | copy-start | bytes 294916
  2.0 18.9 %copy-start.4 = (bf16[2,256,256]{2,1,0:T(8,128)(2,1)S(1)}, bf16[2,256,256]{2,1,0:T(8,128)(2,1)}, u32[]{:S(2)}) copy-start(bf16[2,256,256]{2,1,0:T(8,128)(2,1)} %constant.12.clone.band_ref) | copy-start | bytes 786436
  2.2 18.0 %collective-permute-start = (bf16[624,256]{1,0:T(8,128)(2,1)S(1)}, bf16[624,256]{1,0:T(8,128)(2,1)S(1)}, u32[]{:S(2)}, u32[]{:S(2)}) collective-permute-start(bf16[624,256]{1,0:T(8,128)(2,1)S(1)} %get-tuple-element.9), channel_id=1, source_target_pairs={{0,32},{32,64},{64,96},{96,128},{128,160},{160,192},{192,224},{224... | collective-permute-start | bytes 958472 | tf_op jit(solution)/shard_map/ppermute | solution.py:244
  5.7 15.3 %collective-permute-start.1 = (bf16[624,256]{1,0:T(8,128)(2,1)S(1)}, bf16[624,256]{1,0:T(8,128)(2,1)S(1)}, u32[]{:S(2)}, u32[]{:S(2)}) collective-permute-start(bf16[624,256]{1,0:T(8,128)(2,1)S(1)} %get-tuple-element.10), channel_id=1, source_target_pairs={{32,0},{64,32},{96,64},{128,96},{160,128},{192,160},{224,192},{256... | collective-permute-start | bytes 958472 | tf_op jit(solution)/shard_map/ppermute | solution.py:245
  26.8 36.0 %copy-start.1 = (bf16[256,256]{1,0:T(8,128)(2,1)S(1)}, bf16[256,256]{1,0:T(8,128)(2,1)}, u32[]{:S(2)}) copy-start(bf16[256,256]{1,0:T(8,128)(2,1)} %r_ref.1) | copy-start | bytes 393220

commit v2 on v0

v2 whole, which is shorter than its diff:
```python
import jax
import jax.numpy as jnp
import numpy as np
from jax import lax
from jax.experimental import pallas as pl
from jax.experimental.pallas import tpu as pltpu
from jax.sharding import PartitionSpec as P

STENCIL = (
    -5369.0 / 1800.0,
    12.0 / 7.0,
    -15.0 / 56.0,
    10.0 / 189.0,
    -1.0 / 112.0,
    2.0 / 1925.0,
    -1.0 / 16632.0,
)
CENTRE = 9.0
SPREAD = 7.0
REACH = 6
HALO = 3 * REACH
NEAR = 2 * REACH
TAPS = tuple(-0.5 * s / SPREAD for s in STENCIL)
DIAGONAL = (-CENTRE - 1.5 * STENCIL[0]) / SPREAD
RUN = 4
ROWS = 12
LANES = 128
VMEM_LIMIT = 40 * 1024 * 1024
PACK_LIMIT = 60 * 1024 * 1024
IN_VMEM = pl.BlockSpec(memory_space=pltpu.VMEM)
IN_HBM = pl.BlockSpec(memory_space=pltpu.HBM)


def band_matrices(breadth):
    band = np.zeros((breadth, breadth), np.float64)
    for offset in range(1, REACH + 1):
        band += TAPS[offset] * (np.eye(breadth, k=offset) + np.eye(breadth, k=-offset))
    head = band.astype(jnp.bfloat16)
    rest = (band - head.astype(np.float64)).astype(jnp.bfloat16)
    two = np.asarray(2, jnp.bfloat16)
    return np.stack([head, rest, head * two, rest * two])


def call(kernel, out_shape, in_specs, args, scratch=(), out_specs=None, flops=0, moved=1 << 20, limit=VMEM_LIMIT):
    return pl.pallas_call(
        kernel,
        out_shape=out_shape,
        in_specs=list(in_specs),
        out_specs=jax.tree.map(lambda _: IN_VMEM, out_shape) if out_specs is None else out_specs,
        scratch_shapes=list(scratch),
        compiler_params=pltpu.CompilerParams(vmem_limit_bytes=limit),
        cost_estimate=pl.CostEstimate(flops=flops, bytes_accessed=moved, transcendentals=0),
    )(*args)


def pack(orbitals, potential, layers, height):
    count, cells, breadth = orbitals.shape
    halo_rows = layers * HALO * count
    shape = (halo_rows + layers * NEAR, breadth)

    def kernel(x_hbm, p_hbm, *refs):
        outs, (x_ref, p_ref), held, (sems, out_sems) = refs[:3], refs[3:5], refs[5:8], refs[8:]
        ends = lax.rem(lax.axis_index("grid"), RUN) == RUN - 1
        fetches = [
            pltpu.make_async_copy(x_hbm.at[:, pl.ds(at * height, height), :], x_ref.at[at], sems.at[at])
            for at in range(layers)
        ] + [pltpu.make_async_copy(p_hbm, p_ref, sems.at[layers])]
        for fetch in fetches:
            fetch.start()
        sent = []

        def put(part, here, head, tail):
            for place, rows in enumerate((head, tail, jnp.where(ends, tail, head))):
                held[place][here, :] = rows
            for place in range(3):
                copy = pltpu.make_async_copy(
                    held[place].at[here, :], outs[place].at[here, :], out_sems.at[part, place]
                )
                copy.start()
                sent.append(copy)

        for layer in range(layers):
            fetches[layer].wait()
            own = jnp.concatenate(
                [jnp.swapaxes(x_ref[layer, :, r : r + 8, :], 0, 1) for r in range(0, height, 8)], axis=0
            )
            put(
                layer,
                slice(layer * HALO * count, (layer + 1) * HALO * count),
                own[:HALO].reshape(-1, breadth).astype(jnp.bfloat16),
                own[height - HALO :].reshape(-1, breadth).astype(jnp.bfloat16),
            )
        fetches[layers].wait()
        first, final = (
            jnp.concatenate(
                [p_ref[at * height + r : at * height + r + NEAR, :] for at in range(layers)], axis=0
            ).astype(jnp.bfloat16)
            for r in (0, height - NEAR)
        )
        put(layers, slice(halo_rows, shape[0]), first, final)
        for copy in sent:
            copy.wait()

    halo = jax.ShapeDtypeStruct(shape, jnp.bfloat16)
    return call(
        kernel,
        (halo, halo, halo),
        [IN_HBM] * 2,
        (orbitals, potential),
        scratch=[
            pltpu.VMEM((layers, count, height, breadth), jnp.float32),
            pltpu.VMEM((cells, breadth), jnp.float32),
        ]
        + [pltpu.VMEM(shape, jnp.bfloat16)] * 3
        + [pltpu.SemaphoreType.DMA((layers + 1,)), pltpu.SemaphoreType.DMA((layers + 1, 3))],
        out_specs=(IN_HBM,) * 3,
        limit=PACK_LIMIT,
    )


def dot(a, b):
    return jnp.dot(a, b, preferred_element_type=jnp.float32)


def along_y(u, head, rest):
    u_head = u.astype(jnp.bfloat16)
    u_rest = (u - u_head.astype(jnp.float32)).astype(jnp.bfloat16)
    if JOIN:
        return dot(
            jnp.concatenate([u_head, u_rest, u_head], axis=1), jnp.concatenate([head, head, rest], axis=0)
        )
    return dot(u_head, head) + (dot(u_rest, head) + dot(u_head, rest))


JOIN = True


class Block:
    def __init__(self, count, layers, height, breadth):
        self.count, self.layers, self.height, self.breadth = count, layers, height, breadth
        self.tall = (height + 2 * HALO, height + 2 * NEAR, height + 2 * REACH, height)

    def shape(self, stage):
        return (self.layers * self.tall[stage] * self.count, self.breadth)

    def diagonals(self):
        return (2, self.layers, self.tall[1], self.breadth)

    def at(self, stage, layer, first, size):
        start = (layer * self.tall[stage] + first) * self.count
        return slice(start, start + size * self.count)

    def set_diagonal(self, w, layer, first, potential):
        scaled = potential * (1.0 / SPREAD) + DIAGONAL
        w[0, layer, first : first + potential.shape[0], :] = scaled
        w[1, layer, first : first + potential.shape[0], :] = scaled * 2.0

    def step(self, number, first, size, src, y, w, previous, dst):
        outer = (self.tall[number] - self.height) // 2
        scale = 1.0 if number == 1 else 2.0
        for layer in range(self.layers):
            for lane in range(0, self.breadth, LANES):
                lanes = slice(lane, lane + LANES)

                def rows(ref, stage, at_layer, start, length):
                    return ref[self.at(stage, at_layer, start, length), lanes].reshape(length, self.count, LANES)

                u = rows(src, number - 1, layer, first, size + 2 * REACH)
                start = first + NEAR - outer
                diagonal = jnp.concatenate(
                    [
                        jnp.broadcast_to(w[int(number > 1), layer, start + r : start + r + 1, lanes], (1, self.count, LANES))
                        for r in range(size)
                    ],
                    axis=0,
                )
                total = rows(y, number, layer, first, size) + diagonal * u[REACH : REACH + size]
                for offset in range(1, REACH + 1):
                    low, high = REACH - offset, REACH + offset
                    pair = u[low : low + size] + u[high : high + size]
                    for other in (layer - offset, layer + offset):
                        if 0 <= other < self.layers:
                            pair = pair + rows(src, number - 1, other, first + REACH, size)
                    total = total + (scale * TAPS[offset]) * pair
                if number > 1:
                    total = total - rows(previous, number - 2, layer, first + 2 * REACH, size)
                dst[self.at(number, layer, first, size), lanes] = total.reshape(-1, LANES).astype(dst.dtype)

    def follow(self, number, first, size, src, y, band):
        which = 0 if number == 1 else 2
        for layer in range(self.layers):
            u = src[self.at(number - 1, layer, first + REACH, size), :]
            y[self.at(number, layer, first, size), :] = along_y(u, band[which], band[which + 1])


def prepare(orbitals, potential, band, block):
    height = block.height
    inner = height - 2 * REACH

    def kernel(x_ref, p_ref, band_ref, v0, y1, d1, y2, w):
        for layer in range(block.layers):
            for r in range(0, height, 8):
                first = layer * height + r
                rows = jnp.swapaxes(x_ref[:, first : first + 8, :], 0, 1)
                v0[block.at(0, layer, HALO + r, 8), :] = rows.reshape(-1, block.breadth)
            block.set_diagonal(w, layer, NEAR, p_ref[layer * height : (layer + 1) * height, :])
        block.follow(1, NEAR, height, v0, y1, band_ref)
        block.step(1, NEAR + REACH, inner, v0, y1, w, None, d1)
        block.follow(2, NEAR, inner, d1, y2, band_ref)

    return call(
        kernel,
        tuple(
            jax.ShapeDtypeStruct(s, jnp.float32)
            for s in (block.shape(0), block.shape(1), block.shape(1), block.shape(2), block.diagonals())
        ),
        [IN_VMEM] * 3,
        (orbitals, potential, band),
        flops=6 * 768 * 256 * 256,
        moved=4 << 20,
    )


def filtering(prepared, before, after, wrap, band, block):
    layers, height, count, breadth = block.layers, block.height, block.count, block.breadth
    strips = layers * HALO * count

    def kernel(v0_in, y1_in, d1_in, y2_in, w_in, before_ref, after_ref, wrap_ref, band_ref, out_ref, v0, y1, d1, y2, w, d2, y3):
        place = lax.axis_index("grid")
        in_run = lax.rem(place, RUN)
        opens = (in_run == 0).astype(jnp.float32)
        closes = (in_run == RUN - 1).astype(jnp.float32)

        def sides(source):
            wrapped = wrap_ref[source, :].astype(jnp.float32)
            left = before_ref[source, :].astype(jnp.float32) + opens * wrapped
            return left, after_ref[source, :].astype(jnp.float32) + closes * wrapped

        for layer in range(layers):
            left, right = sides(slice(layer * HALO * count, (layer + 1) * HALO * count))
            v0[block.at(0, layer, 0, HALO), :] = left
            v0[block.at(0, layer, HALO + height, HALO), :] = right
            left, right = sides(slice(strips + layer * NEAR, strips + (layer + 1) * NEAR))
            block.set_diagonal(w, layer, 0, left)
            block.set_diagonal(w, layer, NEAR + height, right)

        def outside(number, ref, at_stage, rows):
            tall = block.tall[at_stage]

            @pl.when(place == 0)
            def _():
                for layer in range(layers):
                    here = block.at(at_stage, layer, 0, rows)
                    ref[here, :] = jnp.zeros((rows * count, breadth), jnp.float32)

            @pl.when(place == lax.axis_size("grid") - 1)
            def _():
                for layer in range(layers):
                    here = block.at(at_stage, layer, tall - rows, rows)
                    ref[here, :] = jnp.zeros((rows * count, breadth), jnp.float32)

        tall = block.tall
        block.follow(1, 0, NEAR, v0, y1, band_ref)
        block.follow(1, NEAR + height, NEAR, v0, y1, band_ref)
        low, high = NEAR + REACH, NEAR + height - REACH
        block.step(1, NEAR, REACH, v0, y1, w, None, d1)
        block.follow(2, REACH, REACH, d1, y2, band_ref)
        block.step(1, high, REACH, v0, y1, w, None, d1)
        block.follow(2, high - REACH, REACH, d1, y2, band_ref)
        block.step(1, 0, NEAR, v0, y1, w, None, d1)
        block.follow(2, 0, REACH, d1, y2, band_ref)
        block.step(1, NEAR + height, NEAR, v0, y1, w, None, d1)
        block.follow(2, REACH + height, REACH, d1, y2, band_ref)
        outside(1, d1, 1, NEAR)
        outside(1, y2, 2, REACH)
        for first in range(0, tall[2], ROWS):
            block.step(2, first, ROWS, d1, y2, w, v0, d2)
            start, stop = max(first, REACH), min(first + ROWS, REACH + height)
            block.follow(3, start - REACH, stop - start, d2, y3, band_ref)
        outside(2, d2, 2, REACH)
        for first in range(0, height, ROWS):
            block.step(3, first, ROWS, d2, y3, w, d1, out_ref)

    f32 = jnp.float32
    out_shape = (jax.ShapeDtypeStruct(block.shape(3), jnp.bfloat16),) + tuple(
        jax.ShapeDtypeStruct(a.shape, f32) for a in prepared
    )
    return pl.pallas_call(
        kernel,
        out_shape=out_shape,
        in_specs=[IN_VMEM] * 9,
        out_specs=(IN_VMEM,) * 6,
        scratch_shapes=[pltpu.VMEM(block.shape(2), f32), pltpu.VMEM(block.shape(3), f32)],
        input_output_aliases={i: i + 1 for i in range(5)},
        compiler_params=pltpu.CompilerParams(vmem_limit_bytes=VMEM_LIMIT),
        cost_estimate=pl.CostEstimate(flops=2 * 3456 * 256 * 768, bytes_accessed=3 << 20, transcendentals=0),
    )(*prepared, before, after, wrap, band)[0]


def rotate(blocks, rotation, parts, per, count):
    rows, breadth = blocks.shape
    total = parts * count

    def kernel(g_ref, r_ref, out_ref):
        cells = g_ref[...].astype(jnp.float32).reshape(parts, per, count, breadth)
        turn = r_ref[...]
        outs = []
        for r in range(per):
            part = cells[:, r].reshape(total, breadth).astype(jnp.bfloat16)
            product = lax.dot_general(
                turn, part, (((0,), (0,)), ((), ())), preferred_element_type=jnp.float32
            )
            outs.append(product.reshape(parts, 1, count, breadth))
        result = jnp.concatenate(outs, axis=1).reshape(rows, breadth)
        out_ref[...] = result.astype(jnp.bfloat16)

    return call(
        kernel,
        jax.ShapeDtypeStruct((rows, breadth), jnp.bfloat16),
        [IN_VMEM, IN_VMEM],
        (blocks, rotation),
        flops=2 * total * rows * breadth,
    )


def unpack(rows, count, layers, height):
    breadth = rows.shape[1]

    def kernel(q_ref, out_hbm, held, sems):
        copies = []
        for layer in range(layers):
            for r in range(0, height, 8):
                first = layer * height + r
                group = q_ref[first * count : (first + 8) * count, :].astype(jnp.float32)
                held[layer, :, r : r + 8, :] = jnp.swapaxes(group.reshape(8, count, breadth), 0, 1)
            copy = pltpu.make_async_copy(
                held.at[layer], out_hbm.at[:, pl.ds(layer * height, height), :], sems.at[layer]
            )
            copy.start()
            copies.append(copy)
        for copy in copies:
            copy.wait()

    return call(
        kernel,
        jax.ShapeDtypeStruct((count, layers * height, breadth), jnp.float32),
        [IN_VMEM],
        (rows,),
        scratch=[
            pltpu.VMEM((layers, count, height, breadth), jnp.float32),
            pltpu.SemaphoreType.DMA((layers,)),
        ],
        out_specs=IN_HBM,
    )


def local(orbitals, potential, rotation):
    count, layers, height, breadth = orbitals.shape
    cells = layers * height
    parts = lax.axis_size("orb")
    columns = lax.axis_size("grid")
    block = Block(count, layers, height, breadth)
    band = jnp.asarray(band_matrices(breadth))
    orbitals = orbitals.reshape(count, cells, breadth)
    potential = potential.reshape(cells, breadth)
    head, tail, wrapped = pack(orbitals, potential, layers, height)
    inner = [i for i in range(columns - 1) if i % RUN != RUN - 1]
    outer = [i for i in range(columns - 1) if i % RUN == RUN - 1]
    before = lax.ppermute(tail, "grid", [(i, i + 1) for i in inner])
    after = lax.ppermute(head, "grid", [(i + 1, i) for i in inner])
    wrap = lax.ppermute(wrapped, "grid", [(i, i + 1) for i in outer] + [(i + 1, i) for i in outer])
    prepared = prepare(orbitals, potential, band, block)
    filtered = filtering(prepared, before, after, wrap, band, block)
    per = cells // parts
    filtered = filtered.reshape(parts, per * count, breadth)
    gathered = lax.all_to_all(filtered, "orb", 0, 0, tiled=True)
    rotated = rotate(gathered.reshape(cells * count, breadth), rotation, parts, per, count)
    returned = lax.all_to_all(rotated.reshape(parts, per * count, breadth), "orb", 0, 0, tiled=True)
    result = unpack(returned.reshape(cells * count, breadth), count, layers, height)
    return result.reshape(count, layers, height, breadth)


def solution(mesh):
    return jax.shard_map(
        local,
        mesh=mesh,
        in_specs=(P("orb", None, "grid", None), P(None, "grid", None), P()),
        out_specs=P("orb", None, "grid", None),
        check_vma=False,
    )
```

time: 252 us -> 82.9 us (0.33)
  waiting for transfers between devices: 196 us -> 7.91 us
  blocking collectives: 0 us -> 51 us
  between operations: 13.5 us -> 0.08 us
  starting transfers between devices: 21.5 us -> 11.6 us
  Pallas kernels: 0 us -> 8.87 us
  other arithmetic: 8.17 us -> 0 us
  matrix products: 6.41 us -> 0 us
    all_gather x1 -> x0, waiting for transfers between devices: 165 us -> none  [local(): lax.all_gather(flattened, 'orb', axis=0, tiled=True)]
    all_to_all x0 -> x2, blocking collectives: none -> 51 us  [the longest x1 28.9 us: local(): gathered = lax.all_to_all(filtered, 'orb', 0, 0, tiled=True)]
    ppermute x6 -> x3, waiting for transfers between devices: 30.3 us -> 7.91 us  [the longest x1 7.91 us: local(): lax.ppermute(wrapped, 'grid', [(i, i + 1) for i in outer] + [(i + 1, i) f...]
    ppermute x6 -> x3, starting transfers between devices: 21.5 us -> 11.6 us  [the longest x1 6.84 us: local(): lax.ppermute(wrapped, 'grid', [(i, i + 1) for i in outer] + [(i + 1, i) f...]
    pallas_call x0 -> x5, Pallas kernels: none -> 8.87 us  [the longest x4 4.49 us: call(): pl.pallas_call(kernel, out_shape=out_shape, in_specs=list(in_specs), out_...]
    dot_general x1 -> x0, matrix products: 6.41 us -> none  [local(): jnp.dot(own_columns.T, lax.all_gather(flattened, 'orb', axis=0, tiled=Tru...]
    convert_element_type x1 -> x0, other arithmetic: 2.78 us -> none  [local(): filtered = filtered.astype(jnp.bfloat16)]
    sub x1 -> x0, other arithmetic: 2.76 us -> none  [chebyshev(): 2.0 * (hamiltonian(current, potential) - centre_value * current)]
  transfers between devices with their start and end apart: 7 -> 3, of which waited for: 7 -> 1; matrix products, arithmetic and copies ran while one was open for 0% -> 0% of each run, Pallas kernels for 0% -> 1%
where the time goes in v2:
time: 82.9 us; the launch traced here: 82.6 us
  blocking collectives  51 us (62%)
  starting transfers between devices  11.6 us (14%)
  Pallas kernels  8.87 us (11%)
  waiting for transfers between devices  7.91 us (10%)
  local copies, waits for them, and re-layouts  3.07 us (4%)
    all_to_all x1, blocking collectives, local(): gathered = lax.all_to_all(filtered, 'orb', 0, 0, tiled=True)  28.9 us
    all_to_all x1, blocking collectives, local(): lax.all_to_all(rotated.reshape(parts, per * count, breadth), 'orb', 0, 0,...  22.1 us
    ppermute x1, waiting for transfers between devices, local(): lax.ppermute(wrapped, 'grid', [(i, i + 1) for i in outer] + [(i + 1, i) f...  7.91 us
    ppermute x1, starting transfers between devices, local(): lax.ppermute(wrapped, 'grid', [(i, i + 1) for i in outer] + [(i + 1, i) f...  6.84 us
    pallas_call x4, Pallas kernels, call(): pl.pallas_call(kernel, out_shape=out_shape, in_specs=list(in_specs), out_...  4.49 us
    pallas_call x1, Pallas kernels, filtering(): pl.pallas_call(kernel, out_shape=out_shape, in_specs=[IN_VMEM] * 9, out_s...  4.38 us
    ppermute x1, starting transfers between devices, local(): before = lax.ppermute(tail, 'grid', [(i, i + 1) for i in inner])  3.5 us
    unnamed x10, local copies, waits for them, and re-layouts  3.07 us
  transfers between devices with their start and end apart: 3, of which 1 were waited for; matrix products, arithmetic and copies ran while one was open for 0% of the time, Pallas kernels for 1%

profile of v2, /device:TPU:6, one launch (start us, length us, event | category | flops | bytes accessed | tf_op | source)
XLA Modules:
  0.0 82.6 jit_solution(6201960225244765215)
XLA Ops:
  0.0 0.0 copy-start.2
  0.0 2.2 %shard_map.47 = (bf16[624,256]{1,0:T(8,128)(2,1)}, bf16[624,256]{1,0:T(8,128)(2,1)}, bf16[624,256]{1,0:T(8,128)(2,1)}) custom-call(f32[8,96,256]{2,1,0:T(8,128)} %bitcast.7, f32[96,256]{1,0:T(8,128)} %bitcast.13), custom_call_target="tpu_custom_call" | custom-call | bytes 1048576 | tf_op jit(solution)/shard_map/pallas_call | solution.py:45
  2.2 3.5 %collective-permute-start = (bf16[624,256]{1,0:T(8,128)(2,1)}, bf16[624,256]{1,0:T(8,128)(2,1)S(1)}, u32[]{:S(2)}, u32[]{:S(2)}) collective-permute-start(bf16[624,256]{1,0:T(8,128)(2,1)} %get-tuple-element.19), channel_id=1, source_target_pairs={{0,32},{32,64},{64,96},{128,160},{160,192},{192,224},{256,288},{28... | collective-permute-start | bytes 958472 | tf_op jit(solution)/shard_map/ppermute | solution.py:369
  5.7 1.3 %collective-permute-start.1 = (bf16[624,256]{1,0:T(8,128)(2,1)}, bf16[624,256]{1,0:T(8,128)(2,1)S(1)}, u32[]{:S(2)}, u32[]{:S(2)}) collective-permute-start(bf16[624,256]{1,0:T(8,128)(2,1)} %get-tuple-element.20), channel_id=1, source_target_pairs={{32,0},{64,32},{96,64},{160,128},{192,160},{224,192},{288,256},{32... | collective-permute-start | bytes 958472 | tf_op jit(solution)/shard_map/ppermute | solution.py:370
  7.0 6.8 %collective-permute-start.2 = (bf16[624,256]{1,0:T(8,128)(2,1)}, bf16[624,256]{1,0:T(8,128)(2,1)S(1)}, u32[]{:S(2)}, u32[]{:S(2)}) collective-permute-start(bf16[624,256]{1,0:T(8,128)(2,1)} %get-tuple-element.21), channel_id=1, source_target_pairs={{96,128},{224,256},{352,384},{128,96},{256,224},{384,352},{97,129}... | collective-permute-start | bytes 958472 | tf_op jit(solution)/shard_map/ppermute | solution.py:371
  13.8 0.0 copy-start
  13.8 1.1 %copy-done = f32[8,4,24,256]{3,2,1,0:T(8,128)S(1)} copy-done((f32[8,4,24,256]{3,2,1,0:T(8,128)S(1)}, f32[8,4,24,256]{3,2,1,0:T(8,128)}, u32[]{:S(2)}) %copy-start) | copy-done | bytes 786456
  15.0 0.0 copy-start.1
  15.0 1.0 %copy-done.1 = bf16[4,256,256]{2,1,0:T(8,128)(2,1)S(1)} copy-done((bf16[4,256,256]{2,1,0:T(8,128)(2,1)S(1)}, bf16[4,256,256]{2,1,0:T(8,128)(2,1)}, u32[]{:S(2)}) %copy-start.1) | copy-done | bytes 524312
  16.0 0.0 copy-start.3
  16.0 0.9 %copy-done.3 = f32[4,24,256]{2,1,0:T(8,128)S(1)} copy-done((f32[4,24,256]{2,1,0:T(8,128)S(1)}, f32[4,24,256]{2,1,0:T(8,128)}, u32[]{:S(2)}) %copy-start.3) | copy-done | bytes 98328
  16.9 1.1 %shard_map.46 = (f32[1920,256]{1,0:T(8,128)S(1)}, f32[1536,256]{1,0:T(8,128)S(1)}, f32[1536,256]{1,0:T(8,128)S(1)}, f32[1152,256]{1,0:T(8,128)S(1)}, f32[2,4,48,256]{3,2,1,0:T(8,128)S(1)}) custom-call(f32[8,96,256]{2,1,0:T(8,128)S(1)} %bitcast.8, f32[96,256]{1,0:T(8,128)S(1)} %bitcast.14, bf16[4,256,256]{2,1,0:T(8,128)(2,1)S(1)} %copy-done.1), custom_call_target="tpu_custom_call" | custom-call | flops 301989888 | bytes 4194304 | tf_op jit(solution)/shard_map/pallas_call | solution.py:45
  18.0 0.0 collective-permute-done.before_ref
  18.0 0.0 collective-permute-done.1.after_ref
  18.0 7.9 %collective-permute-done.2.wrap_ref = bf16[624,256]{1,0:T(8,128)(2,1)S(1)} collective-permute-done((bf16[624,256]{1,0:T(8,128)(2,1)}, bf16[624,256]{1,0:T(8,128)(2,1)S(1)}, u32[]{:S(2)}, u32[]{:S(2)}) %collective-permute-start.2) | collective-permute-done | bytes 319520 | tf_op jit(solution)/shard_map/ppermute | solution.py:371
  25.9 0.0 copy-done.2
  25.9 0.0 copy-start.4
  25.9 4.4 %shard_map.48 = (bf16[768,256]{1,0:T(8,128)(2,1)S(1)}, f32[1920,256]{1,0:T(8,128)S(1)}, f32[1536,256]{1,0:T(8,128)S(1)}, f32[1536,256]{1,0:T(8,128)S(1)}, f32[11...) custom-call(f32[1920,256]{1,0:T(8,128)S(1)} %get-tuple-element.14.v0, ...), custom_call_target="tpu_custom_call", output_to_operand_aliasing={{1}: (0, {}), {2}: (1, {}), {3}: (2, {}), {4}: (3, {}), {5}... | custom-call | flops 1358954496 | bytes 3145728 | tf_op jit(solution)/shard_map/pallas_call | solution.py:288
  30.3 28.9 %all_to_all.10 = bf16[32,24,256]{2,1,0:T(8,128)(2,1)S(1)} all-to-all(bf16[32,24,256]{2,1,0:T(8,128)(2,1)S(1)} %bitcast.12), channel_id=1, replica_groups=mesh['grid'=16,'orb'=32] {'orb'}, dimensions={0} | all-to-all | bytes 786432 | tf_op jit(solution)/shard_map/all_to_all | solution.py:376
  59.2 0.0 copy-done.4
  59.2 0.3 shard_map.49
  59.5 22.1 %all_to_all.11 = bf16[32,24,256]{2,1,0:T(8,128)(2,1)S(1)} all-to-all(bf16[32,24,256]{2,1,0:T(8,128)(2,1)S(1)} %bitcast.10), channel_id=1, replica_groups=mesh['grid'=16,'orb'=32] {'orb'}, dimensions={0} | all-to-all | bytes 786432 | tf_op jit(solution)/shard_map/all_to_all | solution.py:378
  81.6 0.9 %shard_map.50 = f32[8,96,256]{2,1,0:T(8,128)} custom-call(bf16[768,256]{1,0:T(8,128)(2,1)S(1)} %bitcast.11), custom_call_target="tpu_custom_call" | custom-call | bytes 1048576 | tf_op jit(solution)/shard_map/pallas_call | solution.py:45
Async XLA Ops:
  0.0 25.9 %copy-start.2 = (bf16[4,256,256]{2,1,0:T(8,128)(2,1)S(1)}, bf16[4,256,256]{2,1,0:T(8,128)(2,1)}, u32[]{:S(2)}) copy-start(bf16[4,256,256]{2,1,0:T(8,128)(2,1)} %constant.2.clone.band_ref) | copy-start | bytes 1572868
  2.2 15.8 %collective-permute-start = (bf16[624,256]{1,0:T(8,128)(2,1)}, bf16[624,256]{1,0:T(8,128)(2,1)S(1)}, u32[]{:S(2)}, u32[]{:S(2)}) collective-permute-start(bf16[624,256]{1,0:T(8,128)(2,1)} %get-tuple-element.19), channel_id=1, source_target_pairs={{0,32},{32,64},{64,96},{128,160},{160,192},{192,224},{256,288},{28... | collective-permute-start | bytes 958472 | tf_op jit(solution)/shard_map/ppermute | solution.py:369
  5.7 12.3 %collective-permute-start.1 = (bf16[624,256]{1,0:T(8,128)(2,1)}, bf16[624,256]{1,0:T(8,128)(2,1)S(1)}, u32[]{:S(2)}, u32[]{:S(2)}) collective-permute-start(bf16[624,256]{1,0:T(8,128)(2,1)} %get-tuple-element.20), channel_id=1, source_target_pairs={{32,0},{64,32},{96,64},{160,128},{192,160},{224,192},{288,256},{32... | collective-permute-start | bytes 958472 | tf_op jit(solution)/shard_map/ppermute | solution.py:370
  7.0 18.9 %collective-permute-start.2 = (bf16[624,256]{1,0:T(8,128)(2,1)}, bf16[624,256]{1,0:T(8,128)(2,1)S(1)}, u32[]{:S(2)}, u32[]{:S(2)}) collective-permute-start(bf16[624,256]{1,0:T(8,128)(2,1)} %get-tuple-element.21), channel_id=1, source_target_pairs={{96,128},{224,256},{352,384},{128,96},{256,224},{384,352},{97,129}... | collective-permute-start | bytes 958472 | tf_op jit(solution)/shard_map/ppermute | solution.py:371
  13.8 1.1 %copy-start = (f32[8,4,24,256]{3,2,1,0:T(8,128)S(1)}, f32[8,4,24,256]{3,2,1,0:T(8,128)}, u32[]{:S(2)}) copy-start(f32[8,4,24,256]{3,2,1,0:T(8,128)} %param.4) | copy-start | bytes 2359300
  15.0 1.0 %copy-start.1 = (bf16[4,256,256]{2,1,0:T(8,128)(2,1)S(1)}, bf16[4,256,256]{2,1,0:T(8,128)(2,1)}, u32[]{:S(2)}) copy-start(bf16[4,256,256]{2,1,0:T(8,128)(2,1)} %constant.2.clone.band_ref) | copy-start | bytes 1572868
  16.0 0.9 %copy-start.3 = (f32[4,24,256]{2,1,0:T(8,128)S(1)}, f32[4,24,256]{2,1,0:T(8,128)}, u32[]{:S(2)}) copy-start(f32[4,24,256]{2,1,0:T(8,128)} %param.5) | copy-start | bytes 294916
  25.9 33.3 %copy-start.4 = (bf16[256,256]{1,0:T(8,128)(2,1)S(1)}, bf16[256,256]{1,0:T(8,128)(2,1)}, u32[]{:S(2)}) copy-start(bf16[256,256]{1,0:T(8,128)(2,1)} %r_ref.1) | copy-start | bytes 393220

commit v3 on v2

--- a/solution.py
+++ b/solution.py
@@ -26,7 +26,6 @@
 ROWS = 12
 LANES = 128
 VMEM_LIMIT = 40 * 1024 * 1024
-PACK_LIMIT = 60 * 1024 * 1024
 IN_VMEM = pl.BlockSpec(memory_space=pltpu.VMEM)
 IN_HBM = pl.BlockSpec(memory_space=pltpu.HBM)
 
@@ -41,14 +40,14 @@
     return np.stack([head, rest, head * two, rest * two])
 
 
-def call(kernel, out_shape, in_specs, args, scratch=(), out_specs=None, flops=0, moved=1 << 20, limit=VMEM_LIMIT):
+def call(kernel, out_shape, in_specs, args, scratch=(), out_specs=None, flops=0, moved=1 << 20):
     return pl.pallas_call(
         kernel,
         out_shape=out_shape,
         in_specs=list(in_specs),
         out_specs=jax.tree.map(lambda _: IN_VMEM, out_shape) if out_specs is None else out_specs,
         scratch_shapes=list(scratch),
-        compiler_params=pltpu.CompilerParams(vmem_limit_bytes=limit),
+        compiler_params=pltpu.CompilerParams(vmem_limit_bytes=VMEM_LIMIT),
         cost_estimate=pl.CostEstimate(flops=flops, bytes_accessed=moved, transcendentals=0),
     )(*args)
 
@@ -58,8 +57,7 @@
     halo_rows = layers * HALO * count
     shape = (halo_rows + layers * NEAR, breadth)
 
-    def kernel(x_hbm, p_hbm, *refs):
-        outs, (x_ref, p_ref), held, (sems, out_sems) = refs[:3], refs[3:5], refs[5:8], refs[8:]
+    def kernel(x_hbm, p_hbm, head_ref, tail_ref, wrap_ref, x_ref, p_ref, sems):
         ends = lax.rem(lax.axis_index("grid"), RUN) == RUN - 1
         fetches = [
             pltpu.make_async_copy(x_hbm.at[:, pl.ds(at * height, height), :], x_ref.at[at], sems.at[at])
@@ -67,17 +65,11 @@
         ] + [pltpu.make_async_copy(p_hbm, p_ref, sems.at[layers])]
         for fetch in fetches:
             fetch.start()
-        sent = []
-
-        def put(part, here, head, tail):
-            for place, rows in enumerate((head, tail, jnp.where(ends, tail, head))):
-                held[place][here, :] = rows
-            for place in range(3):
-                copy = pltpu.make_async_copy(
-                    held[place].at[here, :], outs[place].at[here, :], out_sems.at[part, place]
-                )
-                copy.start()
-                sent.append(copy)
+
+        def put(here, head, tail):
+            head_ref[here, :] = head
+            tail_ref[here, :] = tail
+            wrap_ref[here, :] = jnp.where(ends, tail, head)
 
         for layer in range(layers):
             fetches[layer].wait()
@@ -85,7 +77,6 @@
                 [jnp.swapaxes(x_ref[layer, :, r : r + 8, :], 0, 1) for r in range(0, height, 8)], axis=0
             )
             put(
-                layer,
                 slice(layer * HALO * count, (layer + 1) * HALO * count),
                 own[:HALO].reshape(-1, breadth).astype(jnp.bfloat16),
                 own[height - HALO :].reshape(-1, breadth).astype(jnp.bfloat16),
@@ -97,24 +88,19 @@
             ).astype(jnp.bfloat16)
             for r in (0, height - NEAR)
         )
-        put(layers, slice(halo_rows, shape[0]), first, final)
-        for copy in sent:
-            copy.wait()
+        put(slice(halo_rows, shape[0]), first, final)
 
     halo = jax.ShapeDtypeStruct(shape, jnp.bfloat16)
     return call(
         kernel,
         (halo, halo, halo),
         [IN_HBM] * 2,
-        (orbitals, potential),
+        [pltpu.with_memory_space_constraint(a, pltpu.HBM) for a in (orbitals, potential)],
         scratch=[
             pltpu.VMEM((layers, count, height, breadth), jnp.float32),
             pltpu.VMEM((cells, breadth), jnp.float32),
-        ]
-        + [pltpu.VMEM(shape, jnp.bfloat16)] * 3
-        + [pltpu.SemaphoreType.DMA((layers + 1,)), pltpu.SemaphoreType.DMA((layers + 1, 3))],
-        out_specs=(IN_HBM,) * 3,
-        limit=PACK_LIMIT,
+            pltpu.SemaphoreType.DMA((layers + 1,)),
+        ],
     )
 
 
@@ -122,17 +108,12 @@
     return jnp.dot(a, b, preferred_element_type=jnp.float32)
 
 
-def along_y(u, head, rest):
+def along_y(u, head, rest, exact):
     u_head = u.astype(jnp.bfloat16)
+    if exact:
+        return dot(jnp.concatenate([u_head, u_head], axis=1), jnp.concatenate([head, rest], axis=0))
     u_rest = (u - u_head.astype(jnp.float32)).astype(jnp.bfloat16)
-    if JOIN:
-        return dot(
-            jnp.concatenate([u_head, u_rest, u_head], axis=1), jnp.concatenate([head, head, rest], axis=0)
-        )
-    return dot(u_head, head) + (dot(u_rest, head) + dot(u_head, rest))
-
-
-JOIN = True
+    return dot(jnp.concatenate([u_head, u_rest, u_head], axis=1), jnp.concatenate([head, head, rest], axis=0))
 
 
 class Block:
@@ -155,7 +136,7 @@
         w[0, layer, first : first + potential.shape[0], :] = scaled
         w[1, layer, first : first + potential.shape[0], :] = scaled * 2.0
 
-    def step(self, number, first, size, src, y, w, previous, dst):
+    def step(self, number, first, size, src, y, w, previous, dst, keep=None):
         outer = (self.tall[number] - self.height) // 2
         scale = 1.0 if number == 1 else 2.0
         for layer in range(self.layers):
@@ -184,13 +165,20 @@
                     total = total + (scale * TAPS[offset]) * pair
                 if number > 1:
                     total = total - rows(previous, number - 2, layer, first + 2 * REACH, size)
+                if keep is not None:
+                    some, scalar = keep
+                    total = jnp.concatenate(
+                        [total[:some] * scalar, total[some:]] if some > 0 else [total[:some], total[some:] * scalar], axis=0
+                    ) if abs(some) < size else total * scalar
                 dst[self.at(number, layer, first, size), lanes] = total.reshape(-1, LANES).astype(dst.dtype)
 
-    def follow(self, number, first, size, src, y, band):
+    def follow(self, number, firsts, size, src, y, band, exact=False):
         which = 0 if number == 1 else 2
-        for layer in range(self.layers):
-            u = src[self.at(number - 1, layer, first + REACH, size), :]
-            y[self.at(number, layer, first, size), :] = along_y(u, band[which], band[which + 1])
+        places = [(layer, first) for first in firsts for layer in range(self.layers)]
+        u = [src[self.at(number - 1, layer, first + REACH, size), :] for layer, first in places]
+        result = along_y(jnp.concatenate(u, axis=0), band[which], band[which + 1], exact)
+        for i, (layer, first) in enumerate(places):
+            y[self.at(number, layer, first, size), :] = result[i * size * self.count : (i + 1) * size * self.count]
 
 
 def prepare(orbitals, potential, band, block):
@@ -204,9 +192,9 @@
                 rows = jnp.swapaxes(x_ref[:, first : first + 8, :], 0, 1)
                 v0[block.at(0, layer, HALO + r, 8), :] = rows.reshape(-1, block.breadth)
             block.set_diagonal(w, layer, NEAR, p_ref[layer * height : (layer + 1) * height, :])
-        block.follow(1, NEAR, height, v0, y1, band_ref)
+        block.follow(1, [NEAR], height, v0, y1, band_ref)
         block.step(1, NEAR + REACH, inner, v0, y1, w, None, d1)
-        block.follow(2, NEAR, inner, d1, y2, band_ref)
+        block.follow(2, [NEAR], inner, d1, y2, band_ref)
 
     return call(
         kernel,
@@ -244,40 +232,23 @@
             block.set_diagonal(w, layer, 0, left)
             block.set_diagonal(w, layer, NEAR + height, right)
 
-        def outside(number, ref, at_stage, rows):
-            tall = block.tall[at_stage]
-
-            @pl.when(place == 0)
-            def _():
-                for layer in range(layers):
-                    here = block.at(at_stage, layer, 0, rows)
-                    ref[here, :] = jnp.zeros((rows * count, breadth), jnp.float32)
-
-            @pl.when(place == lax.axis_size("grid") - 1)
-            def _():
-                for layer in range(layers):
-                    here = block.at(at_stage, layer, tall - rows, rows)
-                    ref[here, :] = jnp.zeros((rows * count, breadth), jnp.float32)
-
+        left = (place > 0).astype(jnp.float32)
+        right = (place < lax.axis_size("grid") - 1).astype(jnp.float32)
         tall = block.tall
-        block.follow(1, 0, NEAR, v0, y1, band_ref)
-        block.follow(1, NEAR + height, NEAR, v0, y1, band_ref)
         low, high = NEAR + REACH, NEAR + height - REACH
-        block.step(1, NEAR, REACH, v0, y1, w, None, d1)
-        block.follow(2, REACH, REACH, d1, y2, band_ref)
-        block.step(1, high, REACH, v0, y1, w, None, d1)
-        block.follow(2, high - REACH, REACH, d1, y2, band_ref)
-        block.step(1, 0, NEAR, v0, y1, w, None, d1)
-        block.follow(2, 0, REACH, d1, y2, band_ref)
-        block.step(1, NEAR + height, NEAR, v0, y1, w, None, d1)
-        block.follow(2, REACH + height, REACH, d1, y2, band_ref)
-        outside(1, d1, 1, NEAR)
-        outside(1, y2, 2, REACH)
+        block.follow(1, [0, NEAR + height], NEAR, v0, y1, band_ref, exact=True)
+        for first in (NEAR, high):
+            block.step(1, first, REACH, v0, y1, w, None, d1)
+            block.follow(2, [first - REACH], REACH, d1, y2, band_ref)
+        block.step(1, 0, NEAR, v0, y1, w, None, d1, (NEAR, left))
+        block.follow(2, [0], REACH, d1, y2, band_ref)
+        block.step(1, NEAR + height, NEAR, v0, y1, w, None, d1, (NEAR, right))
+        block.follow(2, [REACH + height], REACH, d1, y2, band_ref)
         for first in range(0, tall[2], ROWS):
-            block.step(2, first, ROWS, d1, y2, w, v0, d2)
+            keep = {0: (REACH, left), tall[2] - ROWS: (-REACH, right)}.get(first)
+            block.step(2, first, ROWS, d1, y2, w, v0, d2, keep)
             start, stop = max(first, REACH), min(first + ROWS, REACH + height)
-            block.follow(3, start - REACH, stop - start, d2, y3, band_ref)
-        outside(2, d2, 2, REACH)
+            block.follow(3, [start - REACH], stop - start, d2, y3, band_ref)
         for first in range(0, height, ROWS):
             block.step(3, first, ROWS, d2, y3, w, d1, out_ref)
 

time: 82.9 us -> 81.1 us (0.978)
  Pallas kernels: 8.87 us -> 7.29 us
    pallas_call x1, Pallas kernels: 4.38 us -> 3.54 us  [filtering(): pl.pallas_call(kernel, out_shape=out_shape, in_specs=[IN_VMEM] * 9, out_s...]
where the time goes in v3:
time: 81.1 us; the launch traced here: 80.7 us
  blocking collectives  51 us (63%)
  starting transfers between devices  11.6 us (14%)
  waiting for transfers between devices  7.63 us (9%)
  Pallas kernels  7.29 us (9%)
  local copies, waits for them, and re-layouts  3.07 us (4%)
    all_to_all x1, blocking collectives, local(): gathered = lax.all_to_all(filtered, 'orb', 0, 0, tiled=True)  28.9 us
    all_to_all x1, blocking collectives, local(): lax.all_to_all(rotated.reshape(parts, per * count, breadth), 'orb', 0, 0,...  22.1 us
    ppermute x1, waiting for transfers between devices, local(): lax.ppermute(wrapped, 'grid', [(i, i + 1) for i in outer] + [(i + 1, i) f...  7.62 us
    ppermute x1, starting transfers between devices, local(): lax.ppermute(wrapped, 'grid', [(i, i + 1) for i in outer] + [(i + 1, i) f...  6.84 us
    pallas_call x4, Pallas kernels, call(): pl.pallas_call(kernel, out_shape=out_shape, in_specs=list(in_specs), out_...  3.76 us
    pallas_call x1, Pallas kernels, filtering(): pl.pallas_call(kernel, out_shape=out_shape, in_specs=[IN_VMEM] * 9, out_s...  3.54 us
    ppermute x1, starting transfers between devices, local(): before = lax.ppermute(tail, 'grid', [(i, i + 1) for i in inner])  3.5 us
    unnamed x10, local copies, waits for them, and re-layouts  3.07 us
  transfers between devices with their start and end apart: 3, of which 1 were waited for; matrix products, arithmetic and copies ran while one was open for 0% of the time, Pallas kernels for 1%

profile of v3, /device:TPU:6, one launch (start us, length us, event | category | flops | bytes accessed | tf_op | source)
XLA Modules:
  0.0 80.7 jit_solution(4281742437346867427)
XLA Ops:
  0.0 0.0 copy-start.2
  0.0 1.4 %shard_map.47 = (bf16[624,256]{1,0:T(8,128)(2,1)S(1)}, bf16[624,256]{1,0:T(8,128)(2,1)S(1)}, bf16[624,256]{1,0:T(8,128)(2,1)S(1)}) custom-call(f32[8,96,256]{2,1,0:T(8,128)} %bitcast.7, f32[96,256]{1,0:T(8,128)} %bitcast.13), custom_call_target="tpu_custom_call" | custom-call | bytes 1048576 | tf_op jit(solution)/shard_map/pallas_call | solution.py:44
  1.4 3.5 %collective-permute-start = (bf16[624,256]{1,0:T(8,128)(2,1)S(1)}, bf16[624,256]{1,0:T(8,128)(2,1)S(1)}, u32[]{:S(2)}, u32[]{:S(2)}) collective-permute-start(bf16[624,256]{1,0:T(8,128)(2,1)S(1)} %get-tuple-element.19), channel_id=1, source_target_pairs={{0,32},{32,64},{64,96},{128,160},{160,192},{192,224},{256,288},{28... | collective-permute-start | bytes 958472 | tf_op jit(solution)/shard_map/ppermute | solution.py:340
  4.9 1.3 %collective-permute-start.1 = (bf16[624,256]{1,0:T(8,128)(2,1)S(1)}, bf16[624,256]{1,0:T(8,128)(2,1)S(1)}, u32[]{:S(2)}, u32[]{:S(2)}) collective-permute-start(bf16[624,256]{1,0:T(8,128)(2,1)S(1)} %get-tuple-element.20), channel_id=1, source_target_pairs={{32,0},{64,32},{96,64},{160,128},{192,160},{224,192},{288,256},{32... | collective-permute-start | bytes 958472 | tf_op jit(solution)/shard_map/ppermute | solution.py:341
  6.2 6.8 %collective-permute-start.2 = (bf16[624,256]{1,0:T(8,128)(2,1)S(1)}, bf16[624,256]{1,0:T(8,128)(2,1)S(1)}, u32[]{:S(2)}, u32[]{:S(2)}) collective-permute-start(bf16[624,256]{1,0:T(8,128)(2,1)S(1)} %get-tuple-element.21), channel_id=1, source_target_pairs={{96,128},{224,256},{352,384},{128,96},{256,224},{384,352},{97,129}... | collective-permute-start | bytes 958472 | tf_op jit(solution)/shard_map/ppermute | solution.py:342
  13.0 0.0 copy-start
  13.1 1.1 %copy-done = f32[8,4,24,256]{3,2,1,0:T(8,128)S(1)} copy-done((f32[8,4,24,256]{3,2,1,0:T(8,128)S(1)}, f32[8,4,24,256]{3,2,1,0:T(8,128)}, u32[]{:S(2)}) %copy-start) | copy-done | bytes 786456
  14.2 0.0 copy-start.1
  14.2 1.0 %copy-done.1 = bf16[4,256,256]{2,1,0:T(8,128)(2,1)S(1)} copy-done((bf16[4,256,256]{2,1,0:T(8,128)(2,1)S(1)}, bf16[4,256,256]{2,1,0:T(8,128)(2,1)}, u32[]{:S(2)}) %copy-start.1) | copy-done | bytes 524312
  15.2 0.0 copy-start.3
  15.2 0.9 %copy-done.3 = f32[4,24,256]{2,1,0:T(8,128)S(1)} copy-done((f32[4,24,256]{2,1,0:T(8,128)S(1)}, f32[4,24,256]{2,1,0:T(8,128)}, u32[]{:S(2)}) %copy-start.3) | copy-done | bytes 98328
  16.1 1.1 %shard_map.46 = (f32[1920,256]{1,0:T(8,128)S(1)}, f32[1536,256]{1,0:T(8,128)S(1)}, f32[1536,256]{1,0:T(8,128)S(1)}, f32[1152,256]{1,0:T(8,128)S(1)}, f32[2,4,48,256]{3,2,1,0:T(8,128)S(1)}) custom-call(f32[8,96,256]{2,1,0:T(8,128)S(1)} %bitcast.8, f32[96,256]{1,0:T(8,128)S(1)} %bitcast.14, bf16[4,256,256]{2,1,0:T(8,128)(2,1)S(1)} %copy-done.1), custom_call_target="tpu_custom_call" | custom-call | flops 301989888 | bytes 4194304 | tf_op jit(solution)/shard_map/pallas_call | solution.py:44
  17.3 0.0 collective-permute-done.before_ref
  17.3 0.0 collective-permute-done.1.after_ref
  17.3 7.6 %collective-permute-done.2.wrap_ref = bf16[624,256]{1,0:T(8,128)(2,1)S(1)} collective-permute-done((bf16[624,256]{1,0:T(8,128)(2,1)S(1)}, bf16[624,256]{1,0:T(8,128)(2,1)S(1)}, u32[]{:S(2)}, u32[]{:S(2)}) %collective-permute-start.2) | collective-permute-done | bytes 319520 | tf_op jit(solution)/shard_map/ppermute | solution.py:342
  24.9 0.0 copy-done.2
  24.9 0.0 copy-start.4
  24.9 3.5 %shard_map.48 = (bf16[768,256]{1,0:T(8,128)(2,1)S(1)}, f32[1920,256]{1,0:T(8,128)S(1)}, f32[1536,256]{1,0:T(8,128)S(1)}, f32[1536,256]{1,0:T(8,128)S(1)}, f32[11...) custom-call(f32[1920,256]{1,0:T(8,128)S(1)} %get-tuple-element.14.v0, ...), custom_call_target="tpu_custom_call", output_to_operand_aliasing={{1}: (0, {}), {2}: (1, {}), {3}: (2, {}), {4}: (3, {}), {5}... | custom-call | flops 1358954496 | bytes 3145728 | tf_op jit(solution)/shard_map/pallas_call | solution.py:259
  28.4 28.9 %all_to_all.10 = bf16[32,24,256]{2,1,0:T(8,128)(2,1)S(1)} all-to-all(bf16[32,24,256]{2,1,0:T(8,128)(2,1)S(1)} %bitcast.12), channel_id=1, replica_groups=mesh['grid'=16,'orb'=32] {'orb'}, dimensions={0} | all-to-all | bytes 786432 | tf_op jit(solution)/shard_map/all_to_all | solution.py:347
  57.4 0.0 copy-done.4
  57.4 0.3 shard_map.49
  57.7 22.1 %all_to_all.11 = bf16[32,24,256]{2,1,0:T(8,128)(2,1)S(1)} all-to-all(bf16[32,24,256]{2,1,0:T(8,128)(2,1)S(1)} %bitcast.10), channel_id=1, replica_groups=mesh['grid'=16,'orb'=32] {'orb'}, dimensions={0} | all-to-all | bytes 786432 | tf_op jit(solution)/shard_map/all_to_all | solution.py:349
  79.8 0.9 %shard_map.50 = f32[8,96,256]{2,1,0:T(8,128)} custom-call(bf16[768,256]{1,0:T(8,128)(2,1)S(1)} %bitcast.11), custom_call_target="tpu_custom_call" | custom-call | bytes 1048576 | tf_op jit(solution)/shard_map/pallas_call | solution.py:44
Async XLA Ops:
  0.0 24.9 %copy-start.2 = (bf16[4,256,256]{2,1,0:T(8,128)(2,1)S(1)}, bf16[4,256,256]{2,1,0:T(8,128)(2,1)}, u32[]{:S(2)}) copy-start(bf16[4,256,256]{2,1,0:T(8,128)(2,1)} %constant.2.clone.band_ref) | copy-start | bytes 1572868
  1.4 15.9 %collective-permute-start = (bf16[624,256]{1,0:T(8,128)(2,1)S(1)}, bf16[624,256]{1,0:T(8,128)(2,1)S(1)}, u32[]{:S(2)}, u32[]{:S(2)}) collective-permute-start(bf16[624,256]{1,0:T(8,128)(2,1)S(1)} %get-tuple-element.19), channel_id=1, source_target_pairs={{0,32},{32,64},{64,96},{128,160},{160,192},{192,224},{256,288},{28... | collective-permute-start | bytes 958472 | tf_op jit(solution)/shard_map/ppermute | solution.py:340
  4.9 12.4 %collective-permute-start.1 = (bf16[624,256]{1,0:T(8,128)(2,1)S(1)}, bf16[624,256]{1,0:T(8,128)(2,1)S(1)}, u32[]{:S(2)}, u32[]{:S(2)}) collective-permute-start(bf16[624,256]{1,0:T(8,128)(2,1)S(1)} %get-tuple-element.20), channel_id=1, source_target_pairs={{32,0},{64,32},{96,64},{160,128},{192,160},{224,192},{288,256},{32... | collective-permute-start | bytes 958472 | tf_op jit(solution)/shard_map/ppermute | solution.py:341
  6.2 18.7 %collective-permute-start.2 = (bf16[624,256]{1,0:T(8,128)(2,1)S(1)}, bf16[624,256]{1,0:T(8,128)(2,1)S(1)}, u32[]{:S(2)}, u32[]{:S(2)}) collective-permute-start(bf16[624,256]{1,0:T(8,128)(2,1)S(1)} %get-tuple-element.21), channel_id=1, source_target_pairs={{96,128},{224,256},{352,384},{128,96},{256,224},{384,352},{97,129}... | collective-permute-start | bytes 958472 | tf_op jit(solution)/shard_map/ppermute | solution.py:342
  13.0 1.1 %copy-start = (f32[8,4,24,256]{3,2,1,0:T(8,128)S(1)}, f32[8,4,24,256]{3,2,1,0:T(8,128)}, u32[]{:S(2)}) copy-start(f32[8,4,24,256]{3,2,1,0:T(8,128)} %param.4) | copy-start | bytes 2359300
  14.2 1.0 %copy-start.1 = (bf16[4,256,256]{2,1,0:T(8,128)(2,1)S(1)}, bf16[4,256,256]{2,1,0:T(8,128)(2,1)}, u32[]{:S(2)}) copy-start(bf16[4,256,256]{2,1,0:T(8,128)(2,1)} %constant.2.clone.band_ref) | copy-start | bytes 1572868
  15.2 0.9 %copy-start.3 = (f32[4,24,256]{2,1,0:T(8,128)S(1)}, f32[4,24,256]{2,1,0:T(8,128)}, u32[]{:S(2)}) copy-start(f32[4,24,256]{2,1,0:T(8,128)} %param.5) | copy-start | bytes 294916
  24.9 32.5 %copy-start.4 = (bf16[256,256]{1,0:T(8,128)(2,1)S(1)}, bf16[256,256]{1,0:T(8,128)(2,1)}, u32[]{:S(2)}) copy-start(bf16[256,256]{1,0:T(8,128)(2,1)} %r_ref.1) | copy-start | bytes 393220

commit v4 on v3

--- a/solution.py
+++ b/solution.py
@@ -237,20 +237,20 @@
         tall = block.tall
         low, high = NEAR + REACH, NEAR + height - REACH
         block.follow(1, [0, NEAR + height], NEAR, v0, y1, band_ref, exact=True)
-        for first in (NEAR, high):
-            block.step(1, first, REACH, v0, y1, w, None, d1)
-            block.follow(2, [first - REACH], REACH, d1, y2, band_ref)
+        block.step(1, NEAR, REACH, v0, y1, w, None, d1)
+        block.step(1, high, REACH, v0, y1, w, None, d1)
+        block.follow(2, [low - 2 * REACH, high - REACH], REACH, d1, y2, band_ref)
         block.step(1, 0, NEAR, v0, y1, w, None, d1, (NEAR, left))
-        block.follow(2, [0], REACH, d1, y2, band_ref)
         block.step(1, NEAR + height, NEAR, v0, y1, w, None, d1, (NEAR, right))
-        block.follow(2, [REACH + height], REACH, d1, y2, band_ref)
-        for first in range(0, tall[2], ROWS):
-            keep = {0: (REACH, left), tall[2] - ROWS: (-REACH, right)}.get(first)
-            block.step(2, first, ROWS, d1, y2, w, v0, d2, keep)
-            start, stop = max(first, REACH), min(first + ROWS, REACH + height)
-            block.follow(3, [start - REACH], stop - start, d2, y3, band_ref)
-        for first in range(0, height, ROWS):
-            block.step(3, first, ROWS, d2, y3, w, d1, out_ref)
+        block.follow(2, [0, REACH + height], REACH, d1, y2, band_ref)
+        block.step(2, NEAR, height - NEAR, d1, y2, w, v0, d2)
+        block.follow(3, [REACH], height - NEAR, d2, y3, band_ref)
+        block.step(2, 0, NEAR, d1, y2, w, v0, d2, (REACH, left))
+        block.step(2, height, NEAR, d1, y2, w, v0, d2, (-REACH, right))
+        block.follow(3, [0, height - REACH], REACH, d2, y3, band_ref)
+        block.step(3, REACH, height - NEAR, d2, y3, w, d1, out_ref)
+        block.step(3, 0, REACH, d2, y3, w, d1, out_ref)
+        block.step(3, height - REACH, REACH, d2, y3, w, d1, out_ref)
 
     f32 = jnp.float32
     out_shape = (jax.ShapeDtypeStruct(block.shape(3), jnp.bfloat16),) + tuple(

time: 81.1 us -> 80.9 us (level)
  no operation moved by 1% of the time
where the time goes in v4:
time: 80.9 us; the launch traced here: 80.6 us
  blocking collectives  51 us (63%)
  starting transfers between devices  11.6 us (14%)
  waiting for transfers between devices  7.63 us (9%)
  Pallas kernels  7.13 us (9%)
  local copies, waits for them, and re-layouts  3.07 us (4%)
    all_to_all x1, blocking collectives, local(): gathered = lax.all_to_all(filtered, 'orb', 0, 0, tiled=True)  28.9 us
    all_to_all x1, blocking collectives, local(): lax.all_to_all(rotated.reshape(parts, per * count, breadth), 'orb', 0, 0,...  22.1 us
    ppermute x1, waiting for transfers between devices, local(): lax.ppermute(wrapped, 'grid', [(i, i + 1) for i in outer] + [(i + 1, i) f...  7.62 us
    ppermute x1, starting transfers between devices, local(): lax.ppermute(wrapped, 'grid', [(i, i + 1) for i in outer] + [(i + 1, i) f...  6.84 us
    pallas_call x4, Pallas kernels, call(): pl.pallas_call(kernel, out_shape=out_shape, in_specs=list(in_specs), out_...  3.76 us
    ppermute x1, starting transfers between devices, local(): before = lax.ppermute(tail, 'grid', [(i, i + 1) for i in inner])  3.5 us
    pallas_call x1, Pallas kernels, filtering(): pl.pallas_call(kernel, out_shape=out_shape, in_specs=[IN_VMEM] * 9, out_s...  3.37 us
    unnamed x10, local copies, waits for them, and re-layouts  3.07 us
  transfers between devices with their start and end apart: 3, of which 1 were waited for; matrix products, arithmetic and copies ran while one was open for 0% of the time, Pallas kernels for 1%

profile of v4, /device:TPU:6, one launch (start us, length us, event | category | flops | bytes accessed | tf_op | source)
XLA Modules:
  0.0 80.6 jit_solution(4276663167697165668)
XLA Ops:
  0.0 0.0 copy-start.2
  0.0 1.4 %shard_map.47 = (bf16[624,256]{1,0:T(8,128)(2,1)S(1)}, bf16[624,256]{1,0:T(8,128)(2,1)S(1)}, bf16[624,256]{1,0:T(8,128)(2,1)S(1)}) custom-call(f32[8,96,256]{2,1,0:T(8,128)} %bitcast.7, f32[96,256]{1,0:T(8,128)} %bitcast.13), custom_call_target="tpu_custom_call" | custom-call | bytes 1048576 | tf_op jit(solution)/shard_map/pallas_call | solution.py:44
  1.4 3.5 %collective-permute-start = (bf16[624,256]{1,0:T(8,128)(2,1)S(1)}, bf16[624,256]{1,0:T(8,128)(2,1)S(1)}, u32[]{:S(2)}, u32[]{:S(2)}) collective-permute-start(bf16[624,256]{1,0:T(8,128)(2,1)S(1)} %get-tuple-element.19), channel_id=1, source_target_pairs={{0,32},{32,64},{64,96},{128,160},{160,192},{192,224},{256,288},{28... | collective-permute-start | bytes 958472 | tf_op jit(solution)/shard_map/ppermute | solution.py:340
  4.9 1.3 %collective-permute-start.1 = (bf16[624,256]{1,0:T(8,128)(2,1)S(1)}, bf16[624,256]{1,0:T(8,128)(2,1)S(1)}, u32[]{:S(2)}, u32[]{:S(2)}) collective-permute-start(bf16[624,256]{1,0:T(8,128)(2,1)S(1)} %get-tuple-element.20), channel_id=1, source_target_pairs={{32,0},{64,32},{96,64},{160,128},{192,160},{224,192},{288,256},{32... | collective-permute-start | bytes 958472 | tf_op jit(solution)/shard_map/ppermute | solution.py:341
  6.2 6.8 %collective-permute-start.2 = (bf16[624,256]{1,0:T(8,128)(2,1)S(1)}, bf16[624,256]{1,0:T(8,128)(2,1)S(1)}, u32[]{:S(2)}, u32[]{:S(2)}) collective-permute-start(bf16[624,256]{1,0:T(8,128)(2,1)S(1)} %get-tuple-element.21), channel_id=1, source_target_pairs={{96,128},{224,256},{352,384},{128,96},{256,224},{384,352},{97,129}... | collective-permute-start | bytes 958472 | tf_op jit(solution)/shard_map/ppermute | solution.py:342
  13.0 0.0 copy-start
  13.1 1.1 %copy-done = f32[8,4,24,256]{3,2,1,0:T(8,128)S(1)} copy-done((f32[8,4,24,256]{3,2,1,0:T(8,128)S(1)}, f32[8,4,24,256]{3,2,1,0:T(8,128)}, u32[]{:S(2)}) %copy-start) | copy-done | bytes 786456
  14.2 0.0 copy-start.1
  14.2 1.0 %copy-done.1 = bf16[4,256,256]{2,1,0:T(8,128)(2,1)S(1)} copy-done((bf16[4,256,256]{2,1,0:T(8,128)(2,1)S(1)}, bf16[4,256,256]{2,1,0:T(8,128)(2,1)}, u32[]{:S(2)}) %copy-start.1) | copy-done | bytes 524312
  15.2 0.0 copy-start.3
  15.2 0.9 %copy-done.3 = f32[4,24,256]{2,1,0:T(8,128)S(1)} copy-done((f32[4,24,256]{2,1,0:T(8,128)S(1)}, f32[4,24,256]{2,1,0:T(8,128)}, u32[]{:S(2)}) %copy-start.3) | copy-done | bytes 98328
  16.1 1.1 %shard_map.46 = (f32[1920,256]{1,0:T(8,128)S(1)}, f32[1536,256]{1,0:T(8,128)S(1)}, f32[1536,256]{1,0:T(8,128)S(1)}, f32[1152,256]{1,0:T(8,128)S(1)}, f32[2,4,48,256]{3,2,1,0:T(8,128)S(1)}) custom-call(f32[8,96,256]{2,1,0:T(8,128)S(1)} %bitcast.8, f32[96,256]{1,0:T(8,128)S(1)} %bitcast.14, bf16[4,256,256]{2,1,0:T(8,128)(2,1)S(1)} %copy-done.1), custom_call_target="tpu_custom_call" | custom-call | flops 301989888 | bytes 4194304 | tf_op jit(solution)/shard_map/pallas_call | solution.py:44
  17.3 0.0 collective-permute-done.before_ref
  17.3 0.0 collective-permute-done.1.after_ref
  17.3 7.6 %collective-permute-done.2.wrap_ref = bf16[624,256]{1,0:T(8,128)(2,1)S(1)} collective-permute-done((bf16[624,256]{1,0:T(8,128)(2,1)S(1)}, bf16[624,256]{1,0:T(8,128)(2,1)S(1)}, u32[]{:S(2)}, u32[]{:S(2)}) %collective-permute-start.2) | collective-permute-done | bytes 319520 | tf_op jit(solution)/shard_map/ppermute | solution.py:342
  24.9 0.0 copy-done.2
  24.9 0.0 copy-start.4
  24.9 3.4 %shard_map.48 = (bf16[768,256]{1,0:T(8,128)(2,1)S(1)}, f32[1920,256]{1,0:T(8,128)S(1)}, f32[1536,256]{1,0:T(8,128)S(1)}, f32[1536,256]{1,0:T(8,128)S(1)}, f32[11...) custom-call(f32[1920,256]{1,0:T(8,128)S(1)} %get-tuple-element.14.v0, ...), custom_call_target="tpu_custom_call", output_to_operand_aliasing={{1}: (0, {}), {2}: (1, {}), {3}: (2, {}), {4}: (3, {}), {5}... | custom-call | flops 1358954496 | bytes 3145728 | tf_op jit(solution)/shard_map/pallas_call | solution.py:259
  28.3 28.9 %all_to_all.10 = bf16[32,24,256]{2,1,0:T(8,128)(2,1)S(1)} all-to-all(bf16[32,24,256]{2,1,0:T(8,128)(2,1)S(1)} %bitcast.12), channel_id=1, replica_groups=mesh['grid'=16,'orb'=32] {'orb'}, dimensions={0} | all-to-all | bytes 786432 | tf_op jit(solution)/shard_map/all_to_all | solution.py:347
  57.2 0.0 copy-done.4
  57.2 0.3 shard_map.49
  57.5 22.1 %all_to_all.11 = bf16[32,24,256]{2,1,0:T(8,128)(2,1)S(1)} all-to-all(bf16[32,24,256]{2,1,0:T(8,128)(2,1)S(1)} %bitcast.10), channel_id=1, replica_groups=mesh['grid'=16,'orb'=32] {'orb'}, dimensions={0} | all-to-all | bytes 786432 | tf_op jit(solution)/shard_map/all_to_all | solution.py:349
  79.6 0.9 %shard_map.50 = f32[8,96,256]{2,1,0:T(8,128)} custom-call(bf16[768,256]{1,0:T(8,128)(2,1)S(1)} %bitcast.11), custom_call_target="tpu_custom_call" | custom-call | bytes 1048576 | tf_op jit(solution)/shard_map/pallas_call | solution.py:44
Async XLA Ops:
  0.0 24.9 %copy-start.2 = (bf16[4,256,256]{2,1,0:T(8,128)(2,1)S(1)}, bf16[4,256,256]{2,1,0:T(8,128)(2,1)}, u32[]{:S(2)}) copy-start(bf16[4,256,256]{2,1,0:T(8,128)(2,1)} %constant.2.clone.band_ref) | copy-start | bytes 1572868
  1.4 15.9 %collective-permute-start = (bf16[624,256]{1,0:T(8,128)(2,1)S(1)}, bf16[624,256]{1,0:T(8,128)(2,1)S(1)}, u32[]{:S(2)}, u32[]{:S(2)}) collective-permute-start(bf16[624,256]{1,0:T(8,128)(2,1)S(1)} %get-tuple-element.19), channel_id=1, source_target_pairs={{0,32},{32,64},{64,96},{128,160},{160,192},{192,224},{256,288},{28... | collective-permute-start | bytes 958472 | tf_op jit(solution)/shard_map/ppermute | solution.py:340
  4.9 12.4 %collective-permute-start.1 = (bf16[624,256]{1,0:T(8,128)(2,1)S(1)}, bf16[624,256]{1,0:T(8,128)(2,1)S(1)}, u32[]{:S(2)}, u32[]{:S(2)}) collective-permute-start(bf16[624,256]{1,0:T(8,128)(2,1)S(1)} %get-tuple-element.20), channel_id=1, source_target_pairs={{32,0},{64,32},{96,64},{160,128},{192,160},{224,192},{288,256},{32... | collective-permute-start | bytes 958472 | tf_op jit(solution)/shard_map/ppermute | solution.py:341
  6.2 18.7 %collective-permute-start.2 = (bf16[624,256]{1,0:T(8,128)(2,1)S(1)}, bf16[624,256]{1,0:T(8,128)(2,1)S(1)}, u32[]{:S(2)}, u32[]{:S(2)}) collective-permute-start(bf16[624,256]{1,0:T(8,128)(2,1)S(1)} %get-tuple-element.21), channel_id=1, source_target_pairs={{96,128},{224,256},{352,384},{128,96},{256,224},{384,352},{97,129}... | collective-permute-start | bytes 958472 | tf_op jit(solution)/shard_map/ppermute | solution.py:342
  13.0 1.1 %copy-start = (f32[8,4,24,256]{3,2,1,0:T(8,128)S(1)}, f32[8,4,24,256]{3,2,1,0:T(8,128)}, u32[]{:S(2)}) copy-start(f32[8,4,24,256]{3,2,1,0:T(8,128)} %param.4) | copy-start | bytes 2359300
  14.2 1.0 %copy-start.1 = (bf16[4,256,256]{2,1,0:T(8,128)(2,1)S(1)}, bf16[4,256,256]{2,1,0:T(8,128)(2,1)}, u32[]{:S(2)}) copy-start(bf16[4,256,256]{2,1,0:T(8,128)(2,1)} %constant.2.clone.band_ref) | copy-start | bytes 1572868
  15.2 0.9 %copy-start.3 = (f32[4,24,256]{2,1,0:T(8,128)S(1)}, f32[4,24,256]{2,1,0:T(8,128)}, u32[]{:S(2)}) copy-start(f32[4,24,256]{2,1,0:T(8,128)} %param.5) | copy-start | bytes 294916
  24.9 32.3 %copy-start.4 = (bf16[256,256]{1,0:T(8,128)(2,1)S(1)}, bf16[256,256]{1,0:T(8,128)(2,1)}, u32[]{:S(2)}) copy-start(bf16[256,256]{1,0:T(8,128)(2,1)} %r_ref.1) | copy-start | bytes 393220

commit v5 on v4

--- a/solution.py
+++ b/solution.py
@@ -209,63 +209,99 @@
     )
 
 
+def left_side(block, halo, arrays, band, keep):
+    v0, y1, d1, y2, w, d2, y3, out = arrays
+    take_halo(block, halo, v0, w, 0)
+    block.follow(1, [0], NEAR, v0, y1, band, exact=True)
+    block.step(1, NEAR, REACH, v0, y1, w, None, d1)
+    block.step(1, 0, NEAR, v0, y1, w, None, d1, (NEAR, keep))
+    block.follow(2, [0], NEAR, d1, y2, band)
+    block.step(2, NEAR, REACH, d1, y2, w, v0, d2)
+    block.step(2, 0, NEAR, d1, y2, w, v0, d2, (REACH, keep))
+    block.follow(3, [0], NEAR, d2, y3, band)
+    block.step(3, 0, REACH, d2, y3, w, d1, out)
+
+
+def right_side(block, halo, arrays, band, keep):
+    v0, y1, d1, y2, w, d2, y3, out = arrays
+    height = block.height
+    take_halo(block, halo, v0, w, height)
+    block.follow(1, [NEAR + height], NEAR, v0, y1, band, exact=True)
+    block.step(1, NEAR + height - REACH, REACH, v0, y1, w, None, d1)
+    block.step(1, NEAR + height, NEAR, v0, y1, w, None, d1, (NEAR, keep))
+    block.follow(2, [height], NEAR, d1, y2, band)
+    block.step(2, height - REACH, REACH, d1, y2, w, v0, d2)
+    block.step(2, height, NEAR, d1, y2, w, v0, d2, (-REACH, keep))
+    block.follow(3, [height - NEAR], NEAR, d2, y3, band)
+    block.step(3, height - REACH, REACH, d2, y3, w, d1, out)
+
+
+def take_halo(block, halo, v0, w, passed):
+    count, layers = block.count, block.layers
+    past = HALO if passed else 0
+    for layer in range(layers):
+        source = slice(layer * HALO * count, (layer + 1) * HALO * count)
+        v0[block.at(0, layer, past + passed, HALO), :] = halo[source, :].astype(jnp.float32)
+        source = slice(layers * HALO * count + layer * NEAR, layers * HALO * count + (layer + 1) * NEAR)
+        block.set_diagonal(w, layer, passed + (NEAR if passed else 0), halo[source, :].astype(jnp.float32))
+
+
+def filter_call(kernel, block, arrays, extra):
+    given = [a for a in arrays if not isinstance(a, jax.ShapeDtypeStruct)]
+    return pl.pallas_call(
+        kernel,
+        out_shape=tuple(jax.ShapeDtypeStruct(a.shape, a.dtype) for a in arrays),
+        in_specs=[IN_VMEM] * (len(given) + len(extra)),
+        out_specs=(IN_VMEM,) * len(arrays),
+        input_output_aliases={i: i for i in range(len(given))},
+        compiler_params=pltpu.CompilerParams(vmem_limit_bytes=VMEM_LIMIT),
+        cost_estimate=pl.CostEstimate(flops=3456 * 256 * 768, bytes_accessed=3 << 20, transcendentals=0),
+    )(*given, *extra)
+
+
 def filtering(prepared, before, after, wrap, band, block):
-    layers, height, count, breadth = block.layers, block.height, block.count, block.breadth
-    strips = layers * HALO * count
-
-    def kernel(v0_in, y1_in, d1_in, y2_in, w_in, before_ref, after_ref, wrap_ref, band_ref, out_ref, v0, y1, d1, y2, w, d2, y3):
-        place = lax.axis_index("grid")
-        in_run = lax.rem(place, RUN)
-        opens = (in_run == 0).astype(jnp.float32)
-        closes = (in_run == RUN - 1).astype(jnp.float32)
-
-        def sides(source):
-            wrapped = wrap_ref[source, :].astype(jnp.float32)
-            left = before_ref[source, :].astype(jnp.float32) + opens * wrapped
-            return left, after_ref[source, :].astype(jnp.float32) + closes * wrapped
-
-        for layer in range(layers):
-            left, right = sides(slice(layer * HALO * count, (layer + 1) * HALO * count))
-            v0[block.at(0, layer, 0, HALO), :] = left
-            v0[block.at(0, layer, HALO + height, HALO), :] = right
-            left, right = sides(slice(strips + layer * NEAR, strips + (layer + 1) * NEAR))
-            block.set_diagonal(w, layer, 0, left)
-            block.set_diagonal(w, layer, NEAR + height, right)
-
-        left = (place > 0).astype(jnp.float32)
-        right = (place < lax.axis_size("grid") - 1).astype(jnp.float32)
-        tall = block.tall
-        low, high = NEAR + REACH, NEAR + height - REACH
-        block.follow(1, [0, NEAR + height], NEAR, v0, y1, band_ref, exact=True)
-        block.step(1, NEAR, REACH, v0, y1, w, None, d1)
-        block.step(1, high, REACH, v0, y1, w, None, d1)
-        block.follow(2, [low - 2 * REACH, high - REACH], REACH, d1, y2, band_ref)
-        block.step(1, 0, NEAR, v0, y1, w, None, d1, (NEAR, left))
-        block.step(1, NEAR + height, NEAR, v0, y1, w, None, d1, (NEAR, right))
-        block.follow(2, [0, REACH + height], REACH, d1, y2, band_ref)
-        block.step(2, NEAR, height - NEAR, d1, y2, w, v0, d2)
-        block.follow(3, [REACH], height - NEAR, d2, y3, band_ref)
-        block.step(2, 0, NEAR, d1, y2, w, v0, d2, (REACH, left))
-        block.step(2, height, NEAR, d1, y2, w, v0, d2, (-REACH, right))
-        block.follow(3, [0, height - REACH], REACH, d2, y3, band_ref)
-        block.step(3, REACH, height - NEAR, d2, y3, w, d1, out_ref)
-        block.step(3, 0, REACH, d2, y3, w, d1, out_ref)
-        block.step(3, height - REACH, REACH, d2, y3, w, d1, out_ref)
-
-    f32 = jnp.float32
-    out_shape = (jax.ShapeDtypeStruct(block.shape(3), jnp.bfloat16),) + tuple(
-        jax.ShapeDtypeStruct(a.shape, f32) for a in prepared
-    )
-    return pl.pallas_call(
-        kernel,
-        out_shape=out_shape,
-        in_specs=[IN_VMEM] * 9,
-        out_specs=(IN_VMEM,) * 6,
-        scratch_shapes=[pltpu.VMEM(block.shape(2), f32), pltpu.VMEM(block.shape(3), f32)],
-        input_output_aliases={i: i + 1 for i in range(5)},
-        compiler_params=pltpu.CompilerParams(vmem_limit_bytes=VMEM_LIMIT),
-        cost_estimate=pl.CostEstimate(flops=2 * 3456 * 256 * 768, bytes_accessed=3 << 20, transcendentals=0),
-    )(*prepared, before, after, wrap, band)[0]
+    def place():
+        at = lax.axis_index("grid")
+        left = (at > 0).astype(jnp.float32)
+        right = (at < lax.axis_size("grid") - 1).astype(jnp.float32)
+        return lax.rem(at, RUN) == 0, lax.rem(at, RUN) == RUN - 1, left, right
+
+    def early(*refs):
+        before_ref, after_ref, band_ref = refs[5:8]
+        arrays = refs[8:]
+        opens, closes, left, right = place()
+
+        @pl.when(jnp.logical_not(opens))
+        def _():
+            left_side(block, before_ref, arrays, band_ref, left)
+
+        @pl.when(jnp.logical_not(closes))
+        def _():
+            right_side(block, after_ref, arrays, band_ref, right)
+
+    def late(*refs):
+        wrap_ref, band_ref = refs[8:10]
+        arrays = refs[10:]
+        v0, y1, d1, y2, w, d2, y3, out = arrays
+        opens, closes, left, right = place()
+
+        @pl.when(opens)
+        def _():
+            left_side(block, wrap_ref, arrays, band_ref, left)
+
+        @pl.when(closes)
+        def _():
+            right_side(block, wrap_ref, arrays, band_ref, right)
+
+        block.step(3, REACH, block.height - 2 * REACH, d2, y3, w, d1, out)
+
+    made = (
+        jax.ShapeDtypeStruct(block.shape(2), jnp.float32),
+        jax.ShapeDtypeStruct(block.shape(3), jnp.float32),
+        jax.ShapeDtypeStruct(block.shape(3), jnp.bfloat16),
+    )
+    arrays = filter_call(early, block, tuple(prepared) + made, (before, after, band))
+    return filter_call(late, block, arrays, (wrap, band))[-1]
 
 
 def rotate(blocks, rotation, parts, per, count):

time: 80.9 us -> 79.4 us (0.981)
  waiting for transfers between devices: 7.63 us -> 6 us
    ppermute x1, waiting for transfers between devices: 7.62 us -> 6 us  [local(): lax.ppermute(wrapped, 'grid', [(i, i + 1) for i in outer] + [(i + 1, i) f...]
    pallas_call x1 -> x2, Pallas kernels: 3.37 us -> 3.6 us  [filter_call(): pl.pallas_call(kernel, out_shape=tuple((jax.ShapeDtypeStruct(a.shape, a.d...]
    unnamed x10 -> x8, local copies, waits for them, and re-layouts: 3.07 us -> 3.07 us
  transfers between devices with their start and end apart: 3 -> 3, of which waited for: 1 -> 1; matrix products, arithmetic and copies ran while one was open for 0% -> 0% of each run, Pallas kernels for 1% -> 3%
where the time goes in v5:
time: 79.4 us; the launch traced here: 79.1 us
  blocking collectives  51 us (64%)
  starting transfers between devices  11.6 us (15%)
  Pallas kernels  7.27 us (9%)
  waiting for transfers between devices  6 us (8%)
  local copies, waits for them, and re-layouts  3.07 us (4%)
    all_to_all x1, blocking collectives, local(): gathered = lax.all_to_all(filtered, 'orb', 0, 0, tiled=True)  28.9 us
    all_to_all x1, blocking collectives, local(): lax.all_to_all(rotated.reshape(parts, per * count, breadth), 'orb', 0, 0,...  22.1 us
    ppermute x1, starting transfers between devices, local(): lax.ppermute(wrapped, 'grid', [(i, i + 1) for i in outer] + [(i + 1, i) f...  6.84 us
    ppermute x1, waiting for transfers between devices, local(): lax.ppermute(wrapped, 'grid', [(i, i + 1) for i in outer] + [(i + 1, i) f...  6 us
    pallas_call x4, Pallas kernels, call(): pl.pallas_call(kernel, out_shape=out_shape, in_specs=list(in_specs), out_...  3.68 us
    pallas_call x2, Pallas kernels, filter_call(): pl.pallas_call(kernel, out_shape=tuple((jax.ShapeDtypeStruct(a.shape, a.d...  3.6 us
    ppermute x1, starting transfers between devices, local(): before = lax.ppermute(tail, 'grid', [(i, i + 1) for i in inner])  3.5 us
    unnamed x8, local copies, waits for them, and re-layouts  3.07 us
  transfers between devices with their start and end apart: 3, of which 1 were waited for; matrix products, arithmetic and copies ran while one was open for 0% of the time, Pallas kernels for 3%

profile of v5, /device:TPU:6, one launch (start us, length us, event | category | flops | bytes accessed | tf_op | source)
XLA Modules:
  0.0 79.1 jit_solution(6918732452707076309)
XLA Ops:
  0.0 1.3 %shard_map.47 = (bf16[624,256]{1,0:T(8,128)(2,1)S(1)}, bf16[624,256]{1,0:T(8,128)(2,1)S(1)}, bf16[624,256]{1,0:T(8,128)(2,1)S(1)}) custom-call(f32[8,96,256]{2,1,0:T(8,128)} %bitcast.7, f32[96,256]{1,0:T(8,128)} %bitcast.13), custom_call_target="tpu_custom_call" | custom-call | bytes 1048576 | tf_op jit(solution)/shard_map/pallas_call | solution.py:44
  1.3 3.5 %collective-permute-start = (bf16[624,256]{1,0:T(8,128)(2,1)S(1)}, bf16[624,256]{1,0:T(8,128)(2,1)S(1)}, u32[]{:S(2)}, u32[]{:S(2)}) collective-permute-start(bf16[624,256]{1,0:T(8,128)(2,1)S(1)} %get-tuple-element.27), channel_id=1, source_target_pairs={{0,32},{32,64},{64,96},{128,160},{160,192},{192,224},{256,288},{28... | collective-permute-start | bytes 958472 | tf_op jit(solution)/shard_map/ppermute | solution.py:376
  4.8 1.3 %collective-permute-start.1 = (bf16[624,256]{1,0:T(8,128)(2,1)S(1)}, bf16[624,256]{1,0:T(8,128)(2,1)S(1)}, u32[]{:S(2)}, u32[]{:S(2)}) collective-permute-start(bf16[624,256]{1,0:T(8,128)(2,1)S(1)} %get-tuple-element.28), channel_id=1, source_target_pairs={{32,0},{64,32},{96,64},{160,128},{192,160},{224,192},{288,256},{32... | collective-permute-start | bytes 958472 | tf_op jit(solution)/shard_map/ppermute | solution.py:377
  6.1 6.8 %collective-permute-start.2 = (bf16[624,256]{1,0:T(8,128)(2,1)S(1)}, bf16[624,256]{1,0:T(8,128)(2,1)S(1)}, u32[]{:S(2)}, u32[]{:S(2)}) collective-permute-start(bf16[624,256]{1,0:T(8,128)(2,1)S(1)} %get-tuple-element.37), channel_id=1, source_target_pairs={{96,128},{224,256},{352,384},{128,96},{256,224},{384,352},{97,129}... | collective-permute-start | bytes 958472 | tf_op jit(solution)/shard_map/ppermute | solution.py:378
  13.0 0.0 copy-start
  13.0 1.0 %copy-done = bf16[4,256,256]{2,1,0:T(8,128)(2,1)S(1)} copy-done((bf16[4,256,256]{2,1,0:T(8,128)(2,1)S(1)}, bf16[4,256,256]{2,1,0:T(8,128)(2,1)}, u32[]{:S(2)}) %copy-start) | copy-done | bytes 524312
  14.0 0.0 copy-start.1
  14.0 1.1 %copy-done.1 = f32[8,4,24,256]{3,2,1,0:T(8,128)S(1)} copy-done((f32[8,4,24,256]{3,2,1,0:T(8,128)S(1)}, f32[8,4,24,256]{3,2,1,0:T(8,128)}, u32[]{:S(2)}) %copy-start.1) | copy-done | bytes 786456
  15.2 0.0 copy-start.2
  15.2 0.9 %copy-done.2 = f32[4,24,256]{2,1,0:T(8,128)S(1)} copy-done((f32[4,24,256]{2,1,0:T(8,128)S(1)}, f32[4,24,256]{2,1,0:T(8,128)}, u32[]{:S(2)}) %copy-start.2) | copy-done | bytes 98328
  16.1 1.1 %shard_map.46 = (f32[1920,256]{1,0:T(8,128)S(1)}, f32[1536,256]{1,0:T(8,128)S(1)}, f32[1536,256]{1,0:T(8,128)S(1)}, f32[1152,256]{1,0:T(8,128)S(1)}, f32[2,4,48,256]{3,2,1,0:T(8,128)S(1)}) custom-call(f32[8,96,256]{2,1,0:T(8,128)S(1)} %bitcast.8, f32[96,256]{1,0:T(8,128)S(1)} %bitcast.14, bf16[4,256,256]{2,1,0:T(8,128)(2,1)S(1)} %copy-done), custom_call_target="tpu_custom_call" | custom-call | flops 301989888 | bytes 4194304 | tf_op jit(solution)/shard_map/pallas_call | solution.py:44
  17.2 0.0 collective-permute-done.refs_5_
  17.2 0.0 collective-permute-done.1.refs_6_
  17.2 1.7 %shard_map.48 = (f32[1920,256]{1,0:T(8,128)S(1)}, f32[1536,256]{1,0:T(8,128)S(1)}, f32[1536,256]{1,0:T(8,128)S(1)}, f32[1152,256]{1,0:T(8,128)S(1)}, f32[2,4,48,...) custom-call(f32[1920,256]{1,0:T(8,128)S(1)} %get-tuple-element.22.re, ...), custom_call_target="tpu_custom_call", output_to_operand_aliasing={{0}: (0, {}), {1}: (1, {}), {2}: (2, {}), {3}: (3, {}), {4}... | custom-call | flops 679477248 | bytes 3145728 | tf_op jit(solution)/shard_map/pallas_call | solution.py:251
  18.9 6.0 %collective-permute-done.2.refs_8_ = bf16[624,256]{1,0:T(8,128)(2,1)S(1)} collective-permute-done((bf16[624,256]{1,0:T(8,128)(2,1)S(1)}, bf16[624,256]{1,0:T(8,128)(2,1)S(1)}, u32[]{:S(2)}, u32[]{:S(2)}) %collective-permute-start.2) | collective-permute-done | bytes 319520 | tf_op jit(solution)/shard_map/ppermute | solution.py:378
  24.9 0.0 copy-start.3
  24.9 1.9 %shard_map.49 = (f32[1920,256]{1,0:T(8,128)S(1)}, f32[1536,256]{1,0:T(8,128)S(1)}, f32[1536,256]{1,0:T(8,128)S(1)}, f32[1152,256]{1,0:T(8,128)S(1)}, f32[2,4,48,...) custom-call(f32[1920,256]{1,0:T(8,128)S(1)} %get-tuple-element.29.re, ...), custom_call_target="tpu_custom_call", output_to_operand_aliasing={{0}: (0, {}), {1}: (1, {}), {2}: (2, {}), {3}: (3, {}), {4}... | custom-call | flops 679477248 | bytes 3145728 | tf_op jit(solution)/shard_map/pallas_call | solution.py:251
  26.8 28.9 %all_to_all.10 = bf16[32,24,256]{2,1,0:T(8,128)(2,1)S(1)} all-to-all(bf16[32,24,256]{2,1,0:T(8,128)(2,1)S(1)} %bitcast.9), channel_id=1, replica_groups=mesh['grid'=16,'orb'=32] {'orb'}, dimensions={0} | all-to-all | bytes 786432 | tf_op jit(solution)/shard_map/all_to_all | solution.py:383
  55.7 0.0 copy-done.3
  55.7 0.3 shard_map.50
  56.0 22.1 %all_to_all.11 = bf16[32,24,256]{2,1,0:T(8,128)(2,1)S(1)} all-to-all(bf16[32,24,256]{2,1,0:T(8,128)(2,1)S(1)} %bitcast.11), channel_id=1, replica_groups=mesh['grid'=16,'orb'=32] {'orb'}, dimensions={0} | all-to-all | bytes 786432 | tf_op jit(solution)/shard_map/all_to_all | solution.py:385
  78.2 0.9 %shard_map.51 = f32[8,96,256]{2,1,0:T(8,128)} custom-call(bf16[768,256]{1,0:T(8,128)(2,1)S(1)} %bitcast.12), custom_call_target="tpu_custom_call" | custom-call | bytes 1048576 | tf_op jit(solution)/shard_map/pallas_call | solution.py:44
Async XLA Ops:
  1.3 15.8 %collective-permute-start = (bf16[624,256]{1,0:T(8,128)(2,1)S(1)}, bf16[624,256]{1,0:T(8,128)(2,1)S(1)}, u32[]{:S(2)}, u32[]{:S(2)}) collective-permute-start(bf16[624,256]{1,0:T(8,128)(2,1)S(1)} %get-tuple-element.27), channel_id=1, source_target_pairs={{0,32},{32,64},{64,96},{128,160},{160,192},{192,224},{256,288},{28... | collective-permute-start | bytes 958472 | tf_op jit(solution)/shard_map/ppermute | solution.py:376
  4.8 12.3 %collective-permute-start.1 = (bf16[624,256]{1,0:T(8,128)(2,1)S(1)}, bf16[624,256]{1,0:T(8,128)(2,1)S(1)}, u32[]{:S(2)}, u32[]{:S(2)}) collective-permute-start(bf16[624,256]{1,0:T(8,128)(2,1)S(1)} %get-tuple-element.28), channel_id=1, source_target_pairs={{32,0},{64,32},{96,64},{160,128},{192,160},{224,192},{288,256},{32... | collective-permute-start | bytes 958472 | tf_op jit(solution)/shard_map/ppermute | solution.py:377
  6.1 18.7 %collective-permute-start.2 = (bf16[624,256]{1,0:T(8,128)(2,1)S(1)}, bf16[624,256]{1,0:T(8,128)(2,1)S(1)}, u32[]{:S(2)}, u32[]{:S(2)}) collective-permute-start(bf16[624,256]{1,0:T(8,128)(2,1)S(1)} %get-tuple-element.37), channel_id=1, source_target_pairs={{96,128},{224,256},{352,384},{128,96},{256,224},{384,352},{97,129}... | collective-permute-start | bytes 958472 | tf_op jit(solution)/shard_map/ppermute | solution.py:378
  13.0 1.0 %copy-start = (bf16[4,256,256]{2,1,0:T(8,128)(2,1)S(1)}, bf16[4,256,256]{2,1,0:T(8,128)(2,1)}, u32[]{:S(2)}) copy-start(bf16[4,256,256]{2,1,0:T(8,128)(2,1)} %constant.2.clone.band_ref.refs_7_.refs_9_) | copy-start | bytes 1572868
  14.0 1.1 %copy-start.1 = (f32[8,4,24,256]{3,2,1,0:T(8,128)S(1)}, f32[8,4,24,256]{3,2,1,0:T(8,128)}, u32[]{:S(2)}) copy-start(f32[8,4,24,256]{3,2,1,0:T(8,128)} %param.4) | copy-start | bytes 2359300
  15.2 0.9 %copy-start.2 = (f32[4,24,256]{2,1,0:T(8,128)S(1)}, f32[4,24,256]{2,1,0:T(8,128)}, u32[]{:S(2)}) copy-start(f32[4,24,256]{2,1,0:T(8,128)} %param.5) | copy-start | bytes 294916
  24.9 30.9 %copy-start.3 = (bf16[256,256]{1,0:T(8,128)(2,1)S(1)}, bf16[256,256]{1,0:T(8,128)(2,1)}, u32[]{:S(2)}) copy-start(bf16[256,256]{1,0:T(8,128)(2,1)} %r_ref.1) | copy-start | bytes 393220

commit v6 on v5

--- a/solution.py
+++ b/solution.py
@@ -214,11 +214,13 @@
     take_halo(block, halo, v0, w, 0)
     block.follow(1, [0], NEAR, v0, y1, band, exact=True)
     block.step(1, NEAR, REACH, v0, y1, w, None, d1)
+    block.follow(2, [REACH], REACH, d1, y2, band)
     block.step(1, 0, NEAR, v0, y1, w, None, d1, (NEAR, keep))
-    block.follow(2, [0], NEAR, d1, y2, band)
+    block.follow(2, [0], REACH, d1, y2, band)
     block.step(2, NEAR, REACH, d1, y2, w, v0, d2)
-    block.step(2, 0, NEAR, d1, y2, w, v0, d2, (REACH, keep))
+    block.step(2, REACH, REACH, d1, y2, w, v0, d2)
     block.follow(3, [0], NEAR, d2, y3, band)
+    block.step(2, 0, REACH, d1, y2, w, v0, d2, (REACH, keep))
     block.step(3, 0, REACH, d2, y3, w, d1, out)
 
 
@@ -228,22 +230,25 @@
     take_halo(block, halo, v0, w, height)
     block.follow(1, [NEAR + height], NEAR, v0, y1, band, exact=True)
     block.step(1, NEAR + height - REACH, REACH, v0, y1, w, None, d1)
+    block.follow(2, [height], REACH, d1, y2, band)
     block.step(1, NEAR + height, NEAR, v0, y1, w, None, d1, (NEAR, keep))
-    block.follow(2, [height], NEAR, d1, y2, band)
+    block.follow(2, [height + REACH], REACH, d1, y2, band)
     block.step(2, height - REACH, REACH, d1, y2, w, v0, d2)
-    block.step(2, height, NEAR, d1, y2, w, v0, d2, (-REACH, keep))
+    block.step(2, height, REACH, d1, y2, w, v0, d2)
     block.follow(3, [height - NEAR], NEAR, d2, y3, band)
+    block.step(2, height + REACH, REACH, d1, y2, w, v0, d2, (REACH, keep))
     block.step(3, height - REACH, REACH, d2, y3, w, d1, out)
 
 
 def take_halo(block, halo, v0, w, passed):
     count, layers = block.count, block.layers
     past = HALO if passed else 0
+    strips = halo[layers * HALO * count : layers * (HALO * count + NEAR), :].astype(jnp.float32)
     for layer in range(layers):
         source = slice(layer * HALO * count, (layer + 1) * HALO * count)
         v0[block.at(0, layer, past + passed, HALO), :] = halo[source, :].astype(jnp.float32)
-        source = slice(layers * HALO * count + layer * NEAR, layers * HALO * count + (layer + 1) * NEAR)
-        block.set_diagonal(w, layer, passed + (NEAR if passed else 0), halo[source, :].astype(jnp.float32))
+        strip = strips[layer * NEAR : (layer + 1) * NEAR]
+        block.set_diagonal(w, layer, passed + (NEAR if passed else 0), strip)
 
 
 def filter_call(kernel, block, arrays, extra):

time: 79.4 us -> 79.3 us (level)
  no operation moved by 1% of the time
where the time goes in v6:
time: 79.3 us; the launch traced here: 79 us
  blocking collectives  51 us (64%)
  starting transfers between devices  11.6 us (15%)
  Pallas kernels  7.02 us (9%)
  waiting for transfers between devices  6.13 us (8%)
  local copies, waits for them, and re-layouts  3.07 us (4%)
    all_to_all x1, blocking collectives, local(): gathered = lax.all_to_all(filtered, 'orb', 0, 0, tiled=True)  28.9 us
    all_to_all x1, blocking collectives, local(): lax.all_to_all(rotated.reshape(parts, per * count, breadth), 'orb', 0, 0,...  22.1 us
    ppermute x1, starting transfers between devices, local(): lax.ppermute(wrapped, 'grid', [(i, i + 1) for i in outer] + [(i + 1, i) f...  6.84 us
    ppermute x1, waiting for transfers between devices, local(): lax.ppermute(wrapped, 'grid', [(i, i + 1) for i in outer] + [(i + 1, i) f...  6.13 us
    pallas_call x4, Pallas kernels, call(): pl.pallas_call(kernel, out_shape=out_shape, in_specs=list(in_specs), out_...  3.68 us
    ppermute x1, starting transfers between devices, local(): before = lax.ppermute(tail, 'grid', [(i, i + 1) for i in inner])  3.5 us
    pallas_call x2, Pallas kernels, filter_call(): pl.pallas_call(kernel, out_shape=tuple((jax.ShapeDtypeStruct(a.shape, a.d...  3.34 us
    unnamed x8, local copies, waits for them, and re-layouts  3.07 us
  transfers between devices with their start and end apart: 3, of which 1 were waited for; matrix products, arithmetic and copies ran while one was open for 0% of the time, Pallas kernels for 3%

profile of v6, /device:TPU:6, one launch (start us, length us, event | category | flops | bytes accessed | tf_op | source)
XLA Modules:
  0.0 79.0 jit_solution(13839793391240127631)
XLA Ops:
  0.0 1.3 %shard_map.47 = (bf16[624,256]{1,0:T(8,128)(2,1)S(1)}, bf16[624,256]{1,0:T(8,128)(2,1)S(1)}, bf16[624,256]{1,0:T(8,128)(2,1)S(1)}) custom-call(f32[8,96,256]{2,1,0:T(8,128)} %bitcast.7, f32[96,256]{1,0:T(8,128)} %bitcast.13), custom_call_target="tpu_custom_call" | custom-call | bytes 1048576 | tf_op jit(solution)/shard_map/pallas_call | solution.py:44
  1.3 3.5 %collective-permute-start = (bf16[624,256]{1,0:T(8,128)(2,1)S(1)}, bf16[624,256]{1,0:T(8,128)(2,1)S(1)}, u32[]{:S(2)}, u32[]{:S(2)}) collective-permute-start(bf16[624,256]{1,0:T(8,128)(2,1)S(1)} %get-tuple-element.27), channel_id=1, source_target_pairs={{0,32},{32,64},{64,96},{128,160},{160,192},{192,224},{256,288},{28... | collective-permute-start | bytes 958472 | tf_op jit(solution)/shard_map/ppermute | solution.py:381
  4.8 1.3 %collective-permute-start.1 = (bf16[624,256]{1,0:T(8,128)(2,1)S(1)}, bf16[624,256]{1,0:T(8,128)(2,1)S(1)}, u32[]{:S(2)}, u32[]{:S(2)}) collective-permute-start(bf16[624,256]{1,0:T(8,128)(2,1)S(1)} %get-tuple-element.28), channel_id=1, source_target_pairs={{32,0},{64,32},{96,64},{160,128},{192,160},{224,192},{288,256},{32... | collective-permute-start | bytes 958472 | tf_op jit(solution)/shard_map/ppermute | solution.py:382
  6.1 6.8 %collective-permute-start.2 = (bf16[624,256]{1,0:T(8,128)(2,1)S(1)}, bf16[624,256]{1,0:T(8,128)(2,1)S(1)}, u32[]{:S(2)}, u32[]{:S(2)}) collective-permute-start(bf16[624,256]{1,0:T(8,128)(2,1)S(1)} %get-tuple-element.37), channel_id=1, source_target_pairs={{96,128},{224,256},{352,384},{128,96},{256,224},{384,352},{97,129}... | collective-permute-start | bytes 958472 | tf_op jit(solution)/shard_map/ppermute | solution.py:383
  13.0 0.0 copy-start
  13.0 1.0 %copy-done = bf16[4,256,256]{2,1,0:T(8,128)(2,1)S(1)} copy-done((bf16[4,256,256]{2,1,0:T(8,128)(2,1)S(1)}, bf16[4,256,256]{2,1,0:T(8,128)(2,1)}, u32[]{:S(2)}) %copy-start) | copy-done | bytes 524312
  14.0 0.0 copy-start.1
  14.0 1.1 %copy-done.1 = f32[8,4,24,256]{3,2,1,0:T(8,128)S(1)} copy-done((f32[8,4,24,256]{3,2,1,0:T(8,128)S(1)}, f32[8,4,24,256]{3,2,1,0:T(8,128)}, u32[]{:S(2)}) %copy-start.1) | copy-done | bytes 786456
  15.2 0.0 copy-start.2
  15.2 0.9 %copy-done.2 = f32[4,24,256]{2,1,0:T(8,128)S(1)} copy-done((f32[4,24,256]{2,1,0:T(8,128)S(1)}, f32[4,24,256]{2,1,0:T(8,128)}, u32[]{:S(2)}) %copy-start.2) | copy-done | bytes 98328
  16.1 1.1 %shard_map.46 = (f32[1920,256]{1,0:T(8,128)S(1)}, f32[1536,256]{1,0:T(8,128)S(1)}, f32[1536,256]{1,0:T(8,128)S(1)}, f32[1152,256]{1,0:T(8,128)S(1)}, f32[2,4,48,256]{3,2,1,0:T(8,128)S(1)}) custom-call(f32[8,96,256]{2,1,0:T(8,128)S(1)} %bitcast.8, f32[96,256]{1,0:T(8,128)S(1)} %bitcast.14, bf16[4,256,256]{2,1,0:T(8,128)(2,1)S(1)} %copy-done), custom_call_target="tpu_custom_call" | custom-call | flops 301989888 | bytes 4194304 | tf_op jit(solution)/shard_map/pallas_call | solution.py:44
  17.2 0.0 collective-permute-done.refs_5_
  17.2 0.0 collective-permute-done.1.refs_6_
  17.2 1.5 %shard_map.48 = (f32[1920,256]{1,0:T(8,128)S(1)}, f32[1536,256]{1,0:T(8,128)S(1)}, f32[1536,256]{1,0:T(8,128)S(1)}, f32[1152,256]{1,0:T(8,128)S(1)}, f32[2,4,48,...) custom-call(f32[1920,256]{1,0:T(8,128)S(1)} %get-tuple-element.22.re, ...), custom_call_target="tpu_custom_call", output_to_operand_aliasing={{0}: (0, {}), {1}: (1, {}), {2}: (2, {}), {3}: (3, {}), {4}... | custom-call | flops 679477248 | bytes 3145728 | tf_op jit(solution)/shard_map/pallas_call | solution.py:256
  18.7 6.1 %collective-permute-done.2.refs_8_ = bf16[624,256]{1,0:T(8,128)(2,1)S(1)} collective-permute-done((bf16[624,256]{1,0:T(8,128)(2,1)S(1)}, bf16[624,256]{1,0:T(8,128)(2,1)S(1)}, u32[]{:S(2)}, u32[]{:S(2)}) %collective-permute-start.2) | collective-permute-done | bytes 319520 | tf_op jit(solution)/shard_map/ppermute | solution.py:383
  24.9 0.0 copy-start.3
  24.9 1.8 %shard_map.49 = (f32[1920,256]{1,0:T(8,128)S(1)}, f32[1536,256]{1,0:T(8,128)S(1)}, f32[1536,256]{1,0:T(8,128)S(1)}, f32[1152,256]{1,0:T(8,128)S(1)}, f32[2,4,48,...) custom-call(f32[1920,256]{1,0:T(8,128)S(1)} %get-tuple-element.29.re, ...), custom_call_target="tpu_custom_call", output_to_operand_aliasing={{0}: (0, {}), {1}: (1, {}), {2}: (2, {}), {3}: (3, {}), {4}... | custom-call | flops 679477248 | bytes 3145728 | tf_op jit(solution)/shard_map/pallas_call | solution.py:256
  26.7 28.9 %all_to_all.10 = bf16[32,24,256]{2,1,0:T(8,128)(2,1)S(1)} all-to-all(bf16[32,24,256]{2,1,0:T(8,128)(2,1)S(1)} %bitcast.9), channel_id=1, replica_groups=mesh['grid'=16,'orb'=32] {'orb'}, dimensions={0} | all-to-all | bytes 786432 | tf_op jit(solution)/shard_map/all_to_all | solution.py:388
  55.6 0.0 copy-done.3
  55.6 0.3 shard_map.50
  55.9 22.1 %all_to_all.11 = bf16[32,24,256]{2,1,0:T(8,128)(2,1)S(1)} all-to-all(bf16[32,24,256]{2,1,0:T(8,128)(2,1)S(1)} %bitcast.11), channel_id=1, replica_groups=mesh['grid'=16,'orb'=32] {'orb'}, dimensions={0} | all-to-all | bytes 786432 | tf_op jit(solution)/shard_map/all_to_all | solution.py:390
  78.0 0.9 %shard_map.51 = f32[8,96,256]{2,1,0:T(8,128)} custom-call(bf16[768,256]{1,0:T(8,128)(2,1)S(1)} %bitcast.12), custom_call_target="tpu_custom_call" | custom-call | bytes 1048576 | tf_op jit(solution)/shard_map/pallas_call | solution.py:44
Async XLA Ops:
  1.3 15.8 %collective-permute-start = (bf16[624,256]{1,0:T(8,128)(2,1)S(1)}, bf16[624,256]{1,0:T(8,128)(2,1)S(1)}, u32[]{:S(2)}, u32[]{:S(2)}) collective-permute-start(bf16[624,256]{1,0:T(8,128)(2,1)S(1)} %get-tuple-element.27), channel_id=1, source_target_pairs={{0,32},{32,64},{64,96},{128,160},{160,192},{192,224},{256,288},{28... | collective-permute-start | bytes 958472 | tf_op jit(solution)/shard_map/ppermute | solution.py:381
  4.8 12.3 %collective-permute-start.1 = (bf16[624,256]{1,0:T(8,128)(2,1)S(1)}, bf16[624,256]{1,0:T(8,128)(2,1)S(1)}, u32[]{:S(2)}, u32[]{:S(2)}) collective-permute-start(bf16[624,256]{1,0:T(8,128)(2,1)S(1)} %get-tuple-element.28), channel_id=1, source_target_pairs={{32,0},{64,32},{96,64},{160,128},{192,160},{224,192},{288,256},{32... | collective-permute-start | bytes 958472 | tf_op jit(solution)/shard_map/ppermute | solution.py:382
  6.1 18.7 %collective-permute-start.2 = (bf16[624,256]{1,0:T(8,128)(2,1)S(1)}, bf16[624,256]{1,0:T(8,128)(2,1)S(1)}, u32[]{:S(2)}, u32[]{:S(2)}) collective-permute-start(bf16[624,256]{1,0:T(8,128)(2,1)S(1)} %get-tuple-element.37), channel_id=1, source_target_pairs={{96,128},{224,256},{352,384},{128,96},{256,224},{384,352},{97,129}... | collective-permute-start | bytes 958472 | tf_op jit(solution)/shard_map/ppermute | solution.py:383
  13.0 1.0 %copy-start = (bf16[4,256,256]{2,1,0:T(8,128)(2,1)S(1)}, bf16[4,256,256]{2,1,0:T(8,128)(2,1)}, u32[]{:S(2)}) copy-start(bf16[4,256,256]{2,1,0:T(8,128)(2,1)} %constant.2.clone.band_ref.refs_7_.refs_9_) | copy-start | bytes 1572868
  14.0 1.1 %copy-start.1 = (f32[8,4,24,256]{3,2,1,0:T(8,128)S(1)}, f32[8,4,24,256]{3,2,1,0:T(8,128)}, u32[]{:S(2)}) copy-start(f32[8,4,24,256]{3,2,1,0:T(8,128)} %param.4) | copy-start | bytes 2359300
  15.2 0.9 %copy-start.2 = (f32[4,24,256]{2,1,0:T(8,128)S(1)}, f32[4,24,256]{2,1,0:T(8,128)}, u32[]{:S(2)}) copy-start(f32[4,24,256]{2,1,0:T(8,128)} %param.5) | copy-start | bytes 294916
  24.9 30.8 %copy-start.3 = (bf16[256,256]{1,0:T(8,128)(2,1)S(1)}, bf16[256,256]{1,0:T(8,128)(2,1)}, u32[]{:S(2)}) copy-start(bf16[256,256]{1,0:T(8,128)(2,1)} %r_ref.1) | copy-start | bytes 393220
